TPU v7x, 32 devices: a whole 2x2x4 slice. The times are simulated.
32 devices in a mesh: dp: 4 (over x, core), expert: 8 (over z, y).
Axes of the slice: x: 2, y: 2, z: 4, core: 2. Of those that a mesh axis runs over, the one named last changes fastest.
Arguments:
- tokens: bfloat16 [16384, 1024], P(('dp', 'expert')), may hold values from -6 to 6
- doc_lens: int32 [32, 8], P(('dp', 'expert')), may hold values from 0 to 512, as said below
- expert_picks: int32 [16384, 8], P(('dp', 'expert')), may hold values from 0 to 31, all different within a row; in each aligned block of 512 rows (0 to 511, 512 to 1023, ...) at most 192 rows name the same one
- gain_attn: float32 [1024], replicated, may hold values from 0.1 to 1.9
- w_query: bfloat16 [1024, 1024], replicated, may hold values from -0.1875 to 0.1875
- w_key: bfloat16 [1024, 512], replicated, may hold values from -0.1875 to 0.1875
- w_value: bfloat16 [1024, 512], replicated, may hold values from -0.1875 to 0.1875
- w_out: bfloat16 [1024, 1024], replicated, may hold values from -1.5 to 1.5
- gain_ffn: float32 [1024], replicated, may hold values from 0.1 to 1.9
- w_router: bfloat16 [1024, 32], replicated, may hold values from -0.09375 to 0.09375
- w_gate: bfloat16 [32, 1024, 512], P('expert'), may hold values from -0.1875 to 0.1875
- w_up: bfloat16 [32, 1024, 512], P('expert'), may hold values from -0.1875 to 0.1875
- w_down: bfloat16 [32, 512, 1024], P('expert'), may hold values from -0.75 to 0.75
- cotangent: bfloat16 [16384, 1024], P(('dp', 'expert')), may hold values from -6 to 6
Outputs:
- out_tokens: bfloat16 [16384, 1024], P(('dp', 'expert'))
- grad_tokens: bfloat16 [16384, 1024], P(('dp', 'expert'))
- grad_gain_attn: float32 [1024], replicated
- grad_query: float32 [1024, 1024], replicated
- grad_key: float32 [1024, 512], replicated
- grad_value: float32 [1024, 512], replicated
- grad_w_out: float32 [1024, 1024], replicated
- grad_gain_ffn: float32 [1024], replicated
- grad_router: float32 [1024, 32], replicated
- grad_gate: float32 [32, 1024, 512], P('expert', 'dp')
- grad_up: float32 [32, 1024, 512], P('expert', 'dp')
- grad_down: float32 [32, 512, 1024], P('expert', 'dp')
Inputs may be any that keep to these rules, and one draw needn't show every extreme that they name: `doc_lens`: each device's 8 lengths sum to 512; on some device one document fills all 512 tokens. `expert_picks`: A token's 8 experts differ; the rows of one device name one expert at most 192 times, a bound that some block reaches.
All inputs are finite; a program needn't handle non-finite values.
Results may differ from a plain program's by a relative error of at most 0.013.
The roundings to bfloat16 on the way count: a program that leaves them out, or rounds other values in their place, can miss the bound.
Values may be sent and summed in bfloat16 or wider, within the bound.
A program may use at most 256 MiB of HBM per device.

v0:
```python
import jax
import jax.numpy as jnp
from jax import lax
from jax.sharding import PartitionSpec as P

HD = 64
EXPERTS = 32
TOP = 8
CAP = 192


epsilon = 1e-06
theta_base = 10000.0


def doc_layout(lengths, tok_rows):
    ends_at = jnp.cumsum(lengths, dtype=jnp.int32)
    places = jnp.arange(tok_rows, dtype=jnp.int32)
    passed = ends_at[None, :] <= places[:, None]
    segment = jnp.sum(passed.astype(jnp.int32), axis=1, dtype=jnp.int32)
    start_at = jnp.sum(jnp.where(passed, lengths[None, :], 0), axis=1, dtype=jnp.int32)
    return (segment, places - start_at)


def rope_tables(position, head_size):
    freqs = theta_base ** (-2.0 * jnp.arange(head_size // 2, dtype=jnp.float32) / head_size)
    angles = position.astype(jnp.float32)[:, None] * freqs[None, :]
    return (jnp.cos(angles), jnp.sin(angles))


def rotate(field, cosine, sine_part):
    half_width = field.shape[-1] // 2
    first_half = field[..., :half_width]
    second_half = field[..., half_width:]
    cos_b = cosine[:, None, :]
    sin_b = sine_part[:, None, :]
    return jnp.concatenate(
        [first_half * cos_b - second_half * sin_b, second_half * cos_b + first_half * sin_b],
        axis=-1,
    )


def rms_scale(field):
    return lax.rsqrt(jnp.mean(field * field, axis=1, keepdims=True) + epsilon)


def rms_back(field, scale, gain, grad_normed):
    normed = field * scale
    grad_scaled = grad_normed * gain
    grad_field = scale * (
        grad_scaled - normed * jnp.mean(grad_scaled * normed, axis=1, keepdims=True)
    )
    return (grad_field, jnp.sum(grad_normed * normed, axis=0))


def masked_scores(queries, key_rows, allowed):
    scores = (
        jnp.einsum("qgrd,kgd->grqk", queries, key_rows, preferred_element_type=jnp.float32) * 0.125
    )
    return jnp.where(allowed, scores, -1e30)


def slot_table(picks, tok_rows):
    flat_picks = picks.reshape(-1)
    hits = (flat_picks[:, None] == jnp.arange(EXPERTS, dtype=jnp.int32)[None, :]).astype(jnp.int32)
    earlier = jnp.cumsum(hits, axis=0, dtype=jnp.int32) - hits
    ranks = jnp.sum(earlier * hits, axis=1, dtype=jnp.int32)
    slot_of = flat_picks * CAP + ranks
    token_of = jnp.arange(flat_picks.shape[0], dtype=jnp.int32) // TOP
    slot_owner = jnp.full((EXPERTS * CAP,), tok_rows, jnp.int32).at[slot_of].set(token_of)
    return (slot_of, slot_owner)


def expert_forward(arrived, w_gate, w_up):
    gate_pre = jnp.einsum("secd,edf->secf", arrived, w_gate, preferred_element_type=jnp.float32)
    up_pre = jnp.einsum("secd,edf->secf", arrived, w_up, preferred_element_type=jnp.float32)
    hidden = (jax.nn.silu(gate_pre) * up_pre).astype(jnp.bfloat16)
    return (gate_pre, up_pre, hidden)


def shards(
    tokens,
    doc_lens,
    expert_picks,
    gain_attn,
    w_query,
    w_key,
    w_value,
    w_out,
    gain_ffn,
    w_router,
    w_gate,
    w_up,
    w_down,
    cotangent,
):
    tok_rows = tokens.shape[0]
    width = tokens.shape[1]
    local_experts = w_gate.shape[0]
    owner_count = lax.axis_size("expert")
    head_count = w_query.shape[1] // HD
    group_count = w_key.shape[1] // HD
    group_size = head_count // group_count
    segment, position = doc_layout(doc_lens[0], tok_rows)
    cosine, sine_part = rope_tables(position, HD)
    places = jnp.arange(tok_rows, dtype=jnp.int32)
    allowed = (segment[:, None] == segment[None, :]) & (places[None, :] <= places[:, None])
    inputs = tokens.astype(jnp.float32)
    scale_attn = rms_scale(inputs)
    normed_attn = (inputs * scale_attn * gain_attn).astype(jnp.bfloat16)
    queries = rotate(
        jnp.dot(normed_attn, w_query, preferred_element_type=jnp.float32).reshape(
            tok_rows, head_count, HD
        ),
        cosine,
        sine_part,
    )
    queries = queries.astype(jnp.bfloat16).reshape(tok_rows, group_count, group_size, HD)
    key_rows = rotate(
        jnp.dot(normed_attn, w_key, preferred_element_type=jnp.float32).reshape(
            tok_rows, group_count, HD
        ),
        cosine,
        sine_part,
    ).astype(jnp.bfloat16)
    value_rows = (
        jnp.dot(normed_attn, w_value, preferred_element_type=jnp.float32)
        .astype(jnp.bfloat16)
        .reshape(tok_rows, group_count, HD)
    )
    scores = masked_scores(queries, key_rows, allowed)
    maxima = jnp.max(scores, axis=-1, keepdims=True)
    exponent = jnp.exp(scores - maxima)
    totals = jnp.sum(exponent, axis=-1, keepdims=True)
    log_totals = maxima + jnp.log(totals)
    attn_probs = (exponent / totals).astype(jnp.bfloat16)
    attended = jnp.einsum(
        "grqk,kgd->qgrd", attn_probs, value_rows, preferred_element_type=jnp.float32
    )
    attended = attended.reshape(tok_rows, head_count * HD).astype(jnp.bfloat16)
    residual = inputs + jnp.dot(attended, w_out, preferred_element_type=jnp.float32)
    scale_ffn = rms_scale(residual)
    normed_ffn = (residual * scale_ffn * gain_ffn).astype(jnp.bfloat16)
    logits = jnp.dot(normed_ffn, w_router, preferred_element_type=jnp.float32)
    is_chosen = expert_picks[:, :, None] == jnp.arange(EXPERTS, dtype=jnp.int32)[None, None, :]
    chosen = jnp.sum(jnp.where(is_chosen, logits[:, None, :], 0.0), axis=2)
    chosen_exp = jnp.exp(chosen - jnp.max(chosen, axis=1, keepdims=True))
    gate_vals = chosen_exp / jnp.sum(chosen_exp, axis=1, keepdims=True)
    slot_of, slot_owner = slot_table(expert_picks, tok_rows)
    slot_gate = jnp.zeros((EXPERTS * CAP,), jnp.float32).at[slot_of].set(gate_vals.reshape(-1))
    slot_of = slot_of.reshape(tok_rows, TOP)
    padded = jnp.concatenate([normed_ffn, jnp.zeros((1, width), jnp.bfloat16)], axis=0)
    outgoing = padded[slot_owner].reshape(owner_count, local_experts * CAP, width)
    arrived = lax.all_to_all(outgoing, "expert", split_axis=0, concat_axis=0, tiled=True).reshape(
        owner_count, local_experts, CAP, width
    )
    gate_pre, up_pre, hidden = expert_forward(arrived, w_gate, w_up)
    result = jnp.einsum(
        "secf,efd->secd", hidden, w_down, preferred_element_type=jnp.float32
    ).astype(jnp.bfloat16)
    returned = lax.all_to_all(
        result.reshape(owner_count, local_experts * CAP, width),
        "expert",
        split_axis=0,
        concat_axis=0,
        tiled=True,
    )
    returned = returned.reshape(EXPERTS * CAP, width)
    grad_flow = cotangent.astype(jnp.float32)
    expert_sum = jnp.zeros((tok_rows, width), jnp.float32)
    grad_list = []
    for pick_index in range(TOP):
        gathered = returned[slot_of[:, pick_index]].astype(jnp.float32)
        expert_sum = expert_sum + gate_vals[:, pick_index : pick_index + 1] * gathered
        grad_list.append(jnp.sum(grad_flow * gathered, axis=1))
    out_tokens = (residual + expert_sum).astype(jnp.bfloat16)
    grad_gates = jnp.stack(grad_list, axis=1)
    grad_padded = jnp.concatenate([cotangent, jnp.zeros((1, width), jnp.bfloat16)], axis=0)
    slot_grad = (grad_padded[slot_owner].astype(jnp.float32) * slot_gate[:, None]).astype(
        jnp.bfloat16
    )
    slot_grad = slot_grad.reshape(owner_count, local_experts * CAP, width)
    back_grad = lax.all_to_all(slot_grad, "expert", split_axis=0, concat_axis=0, tiled=True)
    back_grad = back_grad.reshape(owner_count, local_experts, CAP, width)
    grad_down = jnp.einsum("secf,secd->efd", hidden, back_grad, preferred_element_type=jnp.float32)
    grad_hidden = jnp.einsum(
        "secd,efd->secf", back_grad, w_down, preferred_element_type=jnp.float32
    )
    sigmoid_gate = jax.nn.sigmoid(gate_pre)
    grad_gate_pre = (
        grad_hidden * up_pre * sigmoid_gate * (1.0 + gate_pre * (1.0 - sigmoid_gate))
    ).astype(jnp.bfloat16)
    grad_up_pre = (grad_hidden * gate_pre * sigmoid_gate).astype(jnp.bfloat16)
    grad_gate = jnp.einsum(
        "secd,secf->edf", arrived, grad_gate_pre, preferred_element_type=jnp.float32
    )
    grad_up = jnp.einsum("secd,secf->edf", arrived, grad_up_pre, preferred_element_type=jnp.float32)
    grad_slots = jnp.einsum(
        "secf,edf->secd", grad_gate_pre, w_gate, preferred_element_type=jnp.float32
    )
    grad_slots = (
        grad_slots
        + jnp.einsum("secf,edf->secd", grad_up_pre, w_up, preferred_element_type=jnp.float32)
    ).astype(jnp.bfloat16)
    grad_rows = lax.all_to_all(
        grad_slots.reshape(owner_count, local_experts * CAP, width),
        "expert",
        split_axis=0,
        concat_axis=0,
        tiled=True,
    )
    grad_rows = grad_rows.reshape(EXPERTS * CAP, width)
    grad_gate, grad_up, grad_down = (
        lax.psum_scatter(
            grad_gate.astype(jnp.bfloat16), "dp", scatter_dimension=1, tiled=True
        ).astype(jnp.float32),
        lax.psum_scatter(
            grad_up.astype(jnp.bfloat16), "dp", scatter_dimension=1, tiled=True
        ).astype(jnp.float32),
        lax.psum_scatter(
            grad_down.astype(jnp.bfloat16), "dp", scatter_dimension=1, tiled=True
        ).astype(jnp.float32),
    )
    grad_chosen = gate_vals * (grad_gates - jnp.sum(gate_vals * grad_gates, axis=1, keepdims=True))
    grad_logits = jnp.sum(jnp.where(is_chosen, grad_chosen[:, :, None], 0.0), axis=1).astype(
        jnp.bfloat16
    )
    grad_router = jnp.einsum(
        "sd,se->de", normed_ffn, grad_logits, preferred_element_type=jnp.float32
    )
    grad_normed_ffn = jnp.einsum(
        "se,de->sd", grad_logits, w_router, preferred_element_type=jnp.float32
    )
    for pick_index in range(TOP):
        grad_normed_ffn = grad_normed_ffn + grad_rows[slot_of[:, pick_index]].astype(jnp.float32)
    grad_norm_part, grad_gain_ffn = rms_back(residual, scale_ffn, gain_ffn, grad_normed_ffn)
    grad_residual = grad_flow + grad_norm_part
    grad_branch = grad_residual.astype(jnp.bfloat16)
    grad_w_out = jnp.einsum("se,sd->ed", attended, grad_branch, preferred_element_type=jnp.float32)
    grad_attended = jnp.einsum("sd,ed->se", grad_branch, w_out, preferred_element_type=jnp.float32)
    grad_attended = grad_attended.astype(jnp.bfloat16).reshape(
        tok_rows, group_count, group_size, HD
    )
    again_probs = jnp.exp(masked_scores(queries, key_rows, allowed) - log_totals)
    grad_probs = jnp.einsum(
        "qgrd,kgd->grqk", grad_attended, value_rows, preferred_element_type=jnp.float32
    )
    grad_scores = (
        again_probs * (grad_probs - jnp.sum(again_probs * grad_probs, axis=-1, keepdims=True))
    ).astype(jnp.bfloat16)
    grad_q = (
        jnp.einsum("grqk,kgd->qgrd", grad_scores, key_rows, preferred_element_type=jnp.float32)
        * 0.125
    )
    grad_k = (
        jnp.einsum("grqk,qgrd->kgd", grad_scores, queries, preferred_element_type=jnp.float32)
        * 0.125
    )
    grad_v = jnp.einsum(
        "grqk,qgrd->kgd",
        again_probs.astype(jnp.bfloat16),
        grad_attended,
        preferred_element_type=jnp.float32,
    )
    grad_q = (
        rotate(grad_q.reshape(tok_rows, head_count, HD), cosine, -sine_part)
        .reshape(tok_rows, head_count * HD)
        .astype(jnp.bfloat16)
    )
    grad_k = (
        rotate(grad_k, cosine, -sine_part).reshape(tok_rows, group_count * HD).astype(jnp.bfloat16)
    )
    grad_v = grad_v.reshape(tok_rows, group_count * HD).astype(jnp.bfloat16)
    grad_query = jnp.einsum("sd,se->de", normed_attn, grad_q, preferred_element_type=jnp.float32)
    grad_key = jnp.einsum("sd,se->de", normed_attn, grad_k, preferred_element_type=jnp.float32)
    grad_value = jnp.einsum("sd,se->de", normed_attn, grad_v, preferred_element_type=jnp.float32)
    grad_normed_attn = jnp.einsum("se,de->sd", grad_q, w_query, preferred_element_type=jnp.float32)
    grad_normed_attn = grad_normed_attn + jnp.einsum(
        "se,de->sd", grad_k, w_key, preferred_element_type=jnp.float32
    )
    grad_normed_attn = grad_normed_attn + jnp.einsum(
        "se,de->sd", grad_v, w_value, preferred_element_type=jnp.float32
    )
    grad_input_part, grad_gain_attn = rms_back(inputs, scale_attn, gain_attn, grad_normed_attn)
    grad_tokens = (grad_residual + grad_input_part).astype(jnp.bfloat16)
    grad_query, grad_key, grad_value, grad_w_out, grad_gain_attn, grad_gain_ffn, grad_router = (
        lax.psum(
            (
                grad_query,
                grad_key,
                grad_value,
                grad_w_out,
                grad_gain_attn,
                grad_gain_ffn,
                grad_router,
            ),
            ("dp", "expert"),
        )
    )
    return (
        out_tokens,
        grad_tokens,
        grad_gain_attn,
        grad_query,
        grad_key,
        grad_value,
        grad_w_out,
        grad_gain_ffn,
        grad_router,
        grad_gate,
        grad_up,
        grad_down,
    )


def solution(mesh):
    placed = (
        P(("dp", "expert"), None),
        P(("dp", "expert"), None),
        P(("dp", "expert"), None),
        P(),
        P(),
        P(),
        P(),
        P(),
        P(),
        P(),
        P("expert", None, None),
        P("expert", None, None),
        P("expert", None, None),
        P(("dp", "expert"), None),
    )
    return jax.shard_map(
        shards,
        mesh=mesh,
        in_specs=placed,
        out_specs=(
            P(("dp", "expert"), None),
            P(("dp", "expert"), None),
            P(),
            P(),
            P(),
            P(),
            P(),
            P(),
            P(),
            P("expert", "dp", None),
            P("expert", "dp", None),
            P("expert", "dp", None),
        ),
        check_vma=False,
    )
```

profile of v0, /device:TPU:0, one launch (start us, length us, event | category | flops | bytes accessed | tf_op | source)
XLA Modules:
  0.0 1847.6 jit_solution(17167729663304306578)
XLA Ops:
  13.4 14.6 reduce-window.19
  35.5 15.7 scatter_custom_fusion
  85.6 26.9 %gather_fusion = bf16[6144,1024]{1,0:T(8,128)(2,1)} fusion(bf16[513,1024]{1,0:T(8,128)(2,1)S(1)} %concatenate.35, s32[6144]{0:T(1024)S(1)} %fusion.100), kind=kCustom, calls=%fused_computation | custom fusion | bytes 25190400 | tf_op jit(solution)/shard_map/gather | solution.py:153
  112.5 280.7 %all_to_all.20 = bf16[8,768,1024]{2,1,0:T(8,128)(2,1)S(1)} all-to-all(bf16[8,768,1024]{2,1,0:T(8,128)(2,1)} %bitcast.223), channel_id=1, replica_groups=mesh['dp'=4,'expert'=8] {'expert'}, dimensions={0} | all-to-all | bytes 25165824 | tf_op jit(solution)/shard_map/all_to_all | solution.py:154
  406.7 17.3 fusion.12
  424.1 10.0 convert_bitcast_fusion
  446.4 26.8 %gather_fusion.9 = bf16[6144,1024]{1,0:T(8,128)(2,1)} fusion(bf16[513,1024]{1,0:T(8,128)(2,1)S(1)} %concatenate.36, s32[6144]{0:T(1024)S(1)} %fusion.100), kind=kCustom, calls=%fused_computation.9 | custom fusion | bytes 25190400 | tf_op jit(solution)/shard_map/gather | solution.py:179
  476.4 240.8 %all-to-all-done.1 = bf16[8,768,1024]{2,1,0:T(8,128)(2,1)} async-done(((bf16[8,768,1024]{2,1,0:T(8,128)(2,1)}), bf16[8,768,1024]{2,1,0:T(8,128)(2,1)}, u32[]{:S(2)}, u32[]{:S(2)}) %all-to-all-start.1) | async-done | bytes 12582944 | tf_op jit(solution)/shard_map/all_to_all | solution.py:161
  726.9 9.7 gather_fusion.7
  736.5 9.8 gather_fusion.6
  746.4 9.7 gather_fusion.5
  775.4 9.8 gather_fusion.2
  785.2 9.8 gather_fusion.1
  800.8 15.7 scatter_custom_fusion.1
  823.5 277.0 %all_to_all.21 = bf16[8,768,1024]{2,1,0:T(8,128)(2,1)} all-to-all(bf16[8,768,1024]{2,1,0:T(8,128)(2,1)S(1)} %fusion), channel_id=1, replica_groups=mesh['dp'=4,'expert'=8] {'expert'}, dimensions={0} | all-to-all | bytes 25165824 | tf_op jit(solution)/shard_map/all_to_all | solution.py:183
  1100.6 22.5 %fusion.11 = (bf16[8,4,192,512]{3,2,0,1:T(8,128)(2,1)}, bf16[8,4,192,512]{3,2,0,1:T(8,128)(2,1)}) fusion(f32[4,8,192,512]{3,2,1,0:T(8,128)} %fusion.23, f32[4,8,192,512]{3,2,1,0:T(8,128)} %get-tuple-element.71, bf16[4,512,1024]{2,1,0:T(8,128)(2,1)} %param.26, bf16[8,4,192,1024]{3,2,1,0:T(8,128)(2,1)} %bitcast.228), kind=kOutput, calls=%fused_computation.41 | convolution fusion | flops 6483345408 | bytes 54525952 | tf_op jit(solution)/shard_map/secd,efd->secf/dot_general | solution.py:186
  1123.0 14.9 fusion.35
  1138.0 19.1 %fusion.6 = bf16[8,4,192,1024]{3,2,0,1:T(8,128)(2,1)} fusion(f32[4,8,192,1024]{3,2,1,0:T(8,128)} %fusion.35, bf16[8,4,192,512]{3,2,0,1:T(8,128)(2,1)} %get-tuple-element.43, bf16[4,1024,512]{2,1,0:T(8,128)(2,1)} %param.25), kind=kOutput, calls=%fused_computation.34 | convolution fusion | flops 6455033856 | bytes 48234496 | tf_op jit(solution)/shard_map/secf,edf->secd/dot_general | solution.py:203
  1157.1 10.7 copy.93
  1173.2 13.8 bitcast_convert_fusion
  1187.0 13.0 bitcast_convert_fusion.1
  1202.3 12.8 bitcast_convert_fusion.2
  1215.2 229.9 %all-to-all-done.3 = bf16[8,768,1024]{2,1,0:T(8,128)(2,1)} async-done(((bf16[8,768,1024]{2,1,0:T(8,128)(2,1)}), bf16[8,768,1024]{2,1,0:T(8,128)(2,1)}, u32[]{:S(2)}, u32[]{:S(2)}) %all-to-all-start.3) | async-done | bytes 12582944 | tf_op jit(solution)/shard_map/all_to_all | solution.py:205
  1454.3 9.7 gather_fusion.16
  1464.0 9.7 gather_fusion.15
  1483.3 10.1 gather_fusion.13
  1493.4 9.7 gather_fusion.12
  1512.8 9.9 gather_fusion.10
  1533.0 15.7 fusion.1
  1548.8 10.9 fusion.3
  1611.5 39.1 %all-reduce.2 = (f32[1024]{0:T(1024)}, f32[1024]{0:T(1024)}) all-reduce(f32[1024]{0:T(1024)S(1)} %get-tuple-element.14, f32[1024]{0:T(1024)S(1)} %get-tuple-element.12), channel_id=1, replica_groups=mesh['dp'=4,'expert'=8] {'dp','expert'}, use_global_device_ids=true, to_apply=%region_29.30 | all-reduce | flops 2048 | bytes 16384 | tf_op jit(solution)/shard_map/psum | solution.py:287
  1654.4 173.0 %all-reduce.6.cloned.1.call-done = (f32[1024,1024]{1,0:T(8,128)}, f32[1024,512]{1,0:T(8,128)}, f32[1024,512]{1,0:T(8,128)}, f32[1024,1024]{1,0:T(8,128)}, f32[1024,32]{0,1:T(8,128)}) async-done(((f32[1024,1024]{1,0:T(8,128)}, f32[1024,512]{1,0:T(8,128)}, f32[1024,512]{1,0:T(8,128)}, f32[1024,1024]{1,0:T(8,128)}, f32[1024,32]{0,1:T(8,128)}), (f32[1024,1024]{1,0:T(8,128)}, f32[1024,512]{1,0:T(8,128)}, ...) | async-done | bytes 12714000 | tf_op jit(solution)/shard_map/psum | solution.py:287
  (268 shorter events, 232.3 us)
Async XLA Ops:
  8.0 73.6 %copy-start = (bf16[1024,1024]{1,0:T(8,128)(2,1)S(1)}, bf16[1024,1024]{1,0:T(8,128)(2,1)}, u32[]{:S(2)}) copy-start(bf16[1024,1024]{1,0:T(8,128)(2,1)} %param.21) | copy-start | bytes 6291460
  10.9 43.5 %copy-start.50 = (f32[512]{0:T(512)}, f32[512]{0:T(512)S(1)}, u32[]{:S(2)}) copy-start(f32[512]{0:T(512)S(1)} %add_rsqrt_fusion.1) | copy-start | bytes 6148
  28.0 23.3 %copy-start.3 = (bf16[512,1024]{1,0:T(8,128)(2,1)S(1)}, bf16[512,1024]{1,0:T(8,128)(2,1)}, u32[]{:S(2)}) copy-start(bf16[512,1024]{1,0:T(8,128)(2,1)} %param.14) | copy-start | bytes 3145732
  28.0 23.3 %copy-start.48 = (f32[1024]{0:T(1024)S(1)}, f32[1024]{0:T(1024)}, u32[]{:S(2)}) copy-start(f32[1024]{0:T(1024)} %param.17) | copy-start | bytes 12292
  35.5 18.9 %copy-start.72 = (s32[4096,1]{0,1:T(1,128)}, s32[4096,1]{0,1:T(1,128)S(1)}, u32[]{:S(2)}) copy-start(s32[4096,1]{0,1:T(1,128)S(1)} %compare_select_fusion.8) | copy-start | bytes 49156
  53.5 20.6 %copy-start.37 = (bf16[512,512]{0,1:T(8,128)(2,1)}, bf16[512,512]{0,1:T(8,128)(2,1)S(1)}, u32[]{:S(2)}) copy-start(bf16[512,512]{0,1:T(8,128)(2,1)S(1)} %convolution_convert_fusion.1) | copy-start | bytes 1572868
  112.5 285.2 %copy-start.73 = (bf16[4,1024,512]{2,1,0:T(8,128)(2,1)S(1)}, bf16[4,1024,512]{2,1,0:T(8,128)(2,1)}, u32[]{:S(2)}) copy-start(bf16[4,1024,512]{2,1,0:T(8,128)(2,1)} %param.24) | copy-start | bytes 12582916
  439.4 277.8 %all-to-all-start.1 = ((bf16[8,768,1024]{2,1,0:T(8,128)(2,1)}), bf16[8,768,1024]{2,1,0:T(8,128)(2,1)}, u32[]{:S(2)}, u32[]{:S(2)}) async-start(bf16[8,768,1024]{2,1,0:T(8,128)(2,1)} %bitcast.221), calls=%async_computation.1 | async-start | bytes 25165824 | tf_op jit(solution)/shard_map/all_to_all | solution.py:161
  446.4 26.9 %copy-start.38 = (bf16[1024,32]{0,1:T(8,128)(2,1)S(1)}, bf16[1024,32]{0,1:T(8,128)(2,1)}, u32[]{:S(2)}) copy-start(bf16[1024,32]{0,1:T(8,128)(2,1)} %param.23) | copy-start | bytes 196612
  446.4 28.5 %copy-start.41 = (s32[512,8]{0,1:T(8,128)S(1)}, s32[512,8]{0,1:T(8,128)}, u32[]{:S(2)}) copy-start(s32[512,8]{0,1:T(8,128)} %param.16) | copy-start | bytes 49156
  476.2 250.6 %copy-start.58 = (s32[1024]{0:T(1024)}, s32[1024]{0:T(1024)S(1)}, u32[]{:S(2)}) copy-start(s32[1024]{0:T(1024)S(1)} %get-tuple-element.76) | copy-start | bytes 12292
  476.2 250.6 %copy-start.56 = (s32[1024]{0:T(1024)}, s32[1024]{0:T(1024)S(1)}, u32[]{:S(2)}) copy-start(s32[1024]{0:T(1024)S(1)} %get-tuple-element.77) | copy-start | bytes 12292
  476.3 260.3 %copy-start.62 = (s32[1024]{0:T(1024)}, s32[1024]{0:T(1024)S(1)}, u32[]{:S(2)}) copy-start(s32[1024]{0:T(1024)S(1)} %get-tuple-element.78) | copy-start | bytes 12292
  476.3 270.1 %copy-start.60 = (s32[1024]{0:T(1024)}, s32[1024]{0:T(1024)S(1)}, u32[]{:S(2)}) copy-start(s32[1024]{0:T(1024)S(1)} %get-tuple-element.79) | copy-start | bytes 12292
  476.3 279.7 %copy-start.66 = (s32[1024]{0:T(1024)}, s32[1024]{0:T(1024)S(1)}, u32[]{:S(2)}) copy-start(s32[1024]{0:T(1024)S(1)} %get-tuple-element.80) | copy-start | bytes 12292
  476.3 289.4 %copy-start.64 = (s32[1024]{0:T(1024)}, s32[1024]{0:T(1024)S(1)}, u32[]{:S(2)}) copy-start(s32[1024]{0:T(1024)S(1)} %get-tuple-element.81) | copy-start | bytes 12292
  476.3 299.0 %copy-start.70 = (s32[1024]{0:T(1024)}, s32[1024]{0:T(1024)S(1)}, u32[]{:S(2)}) copy-start(s32[1024]{0:T(1024)S(1)} %get-tuple-element.82) | copy-start | bytes 12292
  476.3 308.9 %copy-start.68 = (s32[1024]{0:T(1024)}, s32[1024]{0:T(1024)S(1)}, u32[]{:S(2)}) copy-start(s32[1024]{0:T(1024)S(1)} %get-tuple-element.83) | copy-start | bytes 12292
  1167.8 277.4 %all-to-all-start.3 = ((bf16[8,768,1024]{2,1,0:T(8,128)(2,1)}), bf16[8,768,1024]{2,1,0:T(8,128)(2,1)}, u32[]{:S(2)}, u32[]{:S(2)}) async-start(bf16[8,768,1024]{2,1,0:T(8,128)(2,1)} %bitcast.220), calls=%async_computation.3 | async-start | bytes 25165824 | tf_op jit(solution)/shard_map/all_to_all | solution.py:205
  1173.1 423.8 %reduce-scatter.8.cloned.1.call-start = ((), (), s32[]{:S(2)}) async-start(), calls=%async_computation.9 | async-start | bytes 5242880 | tf_op jit(solution)/shard_map/reduce_scatter | solution.py:220
  1187.0 412.7 %reduce-scatter.6.cloned.1.call-start = ((), (), s32[]{:S(2)}) async-start(), calls=%async_computation.8 | async-start | bytes 5242880 | tf_op jit(solution)/shard_map/reduce_scatter | solution.py:217
  1200.1 402.4 %reduce-scatter.4.cloned.1.call-start = ((), (), s32[]{:S(2)}) async-start(), calls=%async_computation.7 | async-start | bytes 5242880 | tf_op jit(solution)/shard_map/reduce_scatter | solution.py:214
  1215.1 230.0 %copy-start.59 = (s32[1024]{0:T(1024)S(1)}, s32[1024]{0:T(1024)}, u32[]{:S(2)}) copy-start(s32[1024]{0:T(1024)} %copy-done.58) | copy-start | bytes 12292
  1215.2 612.2 %all-reduce.6.cloned.1.call-start = ((), (), s32[]{:S(2)}) async-start(), calls=%async_computation.10 | async-start | bytes 25427968 | tf_op jit(solution)/shard_map/psum | solution.py:287
  1483.3 10.1 copy-start.65
  1512.8 9.9 copy-start.55
  1533.0 15.7 slice-start
  1533.0 15.7 slice-start.1
  1533.0 15.7 slice-start.2
  1533.0 15.8 slice-start.3
  1548.8 10.9 copy-start.20
  1548.8 10.9 copy-start.22
  (54 other events, 235.6 us)
Sparse Core Ops, SparseCore 0:
  1187.1 45.7 reduce-scatter.7
  1235.6 44.5 reduce-scatter.5
  1282.7 44.4 reduce-scatter.3
Sparse Core Ops, SparseCore 1:
  1591.2 236.1 all-reduce.5
where the time goes:
time: 1850 us
  waiting for transfers between devices  644 us (35%)
  blocking collectives  597 us (32%)
  local copies, waits for them, and re-layouts  289 us (16%)
  matrix products  212 us (11%)
  other arithmetic  78.1 us (4%)
    all_to_all x1, blocking collectives, shards(): lax.all_to_all(outgoing, 'expert', split_axis=0, concat_axis=0, tiled=True)  281 us
    all_to_all x1, blocking collectives, shards(): lax.all_to_all(slot_grad, 'expert', split_axis=0, concat_axis=0, tiled=True)  277 us
    all_to_all x1, waiting for transfers between devices, shards(): lax.all_to_all(result.reshape(owner_count, local_experts * CAP, width), '...  241 us
    all_to_all x1, waiting for transfers between devices, shards(): lax.all_to_all(grad_slots.reshape(owner_count, local_experts * CAP, width...  230 us
    psum x1, waiting for transfers between devices, shards(): lax.psum((grad_query, grad_key, grad_value, grad_w_out, grad_gain_attn, g...  173 us
    gather x8, local copies, waits for them, and re-layouts, shards(): gathered = returned[slot_of[:, pick_index]].astype(jnp.float32)  77.7 us
    gather x8, local copies, waits for them, and re-layouts, shards(): grad_rows[slot_of[:, pick_index]].astype(jnp.float32)  77.5 us
    psum x1, blocking collectives, shards(): lax.psum((grad_query, grad_key, grad_value, grad_w_out, grad_gain_attn, g...  39.1 us
  transfers between devices with their start and end apart: 6, of which 3 were waited for; matrix products, arithmetic and copies ran while one was open for 13% of the time, Pallas kernels for 0%

commit v1 on v0

--- a/solution.py
+++ b/solution.py
@@ -58,17 +58,6 @@
         jnp.einsum("qgrd,kgd->grqk", queries, key_rows, preferred_element_type=jnp.float32) * 0.125
     )
     return jnp.where(allowed, scores, -1e30)
-
-
-def slot_table(picks, tok_rows):
-    flat_picks = picks.reshape(-1)
-    hits = (flat_picks[:, None] == jnp.arange(EXPERTS, dtype=jnp.int32)[None, :]).astype(jnp.int32)
-    earlier = jnp.cumsum(hits, axis=0, dtype=jnp.int32) - hits
-    ranks = jnp.sum(earlier * hits, axis=1, dtype=jnp.int32)
-    slot_of = flat_picks * CAP + ranks
-    token_of = jnp.arange(flat_picks.shape[0], dtype=jnp.int32) // TOP
-    slot_owner = jnp.full((EXPERTS * CAP,), tok_rows, jnp.int32).at[slot_of].set(token_of)
-    return (slot_of, slot_owner)
 
 
 def expert_forward(arrived, w_gate, w_up):
@@ -101,6 +90,9 @@
     head_count = w_query.shape[1] // HD
     group_count = w_key.shape[1] // HD
     group_size = head_count // group_count
+    owner = lax.axis_index("expert")
+    cot_all = lax.all_gather(cotangent, "expert")
+    picks_all = lax.all_gather(expert_picks.T, "expert")
     segment, position = doc_layout(doc_lens[0], tok_rows)
     cosine, sine_part = rope_tables(position, HD)
     places = jnp.arange(tok_rows, dtype=jnp.int32)
@@ -141,48 +133,52 @@
     residual = inputs + jnp.dot(attended, w_out, preferred_element_type=jnp.float32)
     scale_ffn = rms_scale(residual)
     normed_ffn = (residual * scale_ffn * gain_ffn).astype(jnp.bfloat16)
-    logits = jnp.dot(normed_ffn, w_router, preferred_element_type=jnp.float32)
-    is_chosen = expert_picks[:, :, None] == jnp.arange(EXPERTS, dtype=jnp.int32)[None, None, :]
-    chosen = jnp.sum(jnp.where(is_chosen, logits[:, None, :], 0.0), axis=2)
-    chosen_exp = jnp.exp(chosen - jnp.max(chosen, axis=1, keepdims=True))
-    gate_vals = chosen_exp / jnp.sum(chosen_exp, axis=1, keepdims=True)
-    slot_of, slot_owner = slot_table(expert_picks, tok_rows)
-    slot_gate = jnp.zeros((EXPERTS * CAP,), jnp.float32).at[slot_of].set(gate_vals.reshape(-1))
-    slot_of = slot_of.reshape(tok_rows, TOP)
-    padded = jnp.concatenate([normed_ffn, jnp.zeros((1, width), jnp.bfloat16)], axis=0)
-    outgoing = padded[slot_owner].reshape(owner_count, local_experts * CAP, width)
-    arrived = lax.all_to_all(outgoing, "expert", split_axis=0, concat_axis=0, tiled=True).reshape(
-        owner_count, local_experts, CAP, width
-    )
+    normed_all = lax.all_gather(normed_ffn, "expert")
+    earlier = (places[:, None] < places[None, :]).astype(jnp.bfloat16)
+    expert_ids = jnp.arange(EXPERTS, dtype=jnp.int32)
+    chosen = jnp.any(picks_all[:, :, None, :] == expert_ids[None, None, :, None], axis=1)
+    own_ids = owner * local_experts
+    hits = lax.dynamic_slice_in_dim(chosen, own_ids, local_experts, axis=1)
+    ranks = jnp.einsum(
+        "set,tu->seu", hits.astype(jnp.bfloat16), earlier, preferred_element_type=jnp.float32
+    ).astype(jnp.int32)
+    ranks = jnp.where(hits, ranks, -1)
+    takes = ranks[:, :, None, :] == jnp.arange(CAP, dtype=jnp.int32)[None, None, :, None]
+    one_hot = takes.astype(jnp.bfloat16)
+    grad_taken = jnp.einsum(
+        "sect,std->secd", one_hot, cot_all, preferred_element_type=jnp.float32
+    ).astype(jnp.bfloat16)
+    logits = jnp.einsum("std,de->set", normed_all, w_router, preferred_element_type=jnp.float32)
+    logits = jnp.where(chosen, logits, -1e30)
+    gate_exp = jnp.exp(logits - jnp.max(logits, axis=1, keepdims=True))
+    gate_exp = jnp.where(chosen, gate_exp, 0.0)
+    gates = gate_exp / jnp.sum(gate_exp, axis=1, keepdims=True)
+    own_gates = lax.dynamic_slice_in_dim(gates, own_ids, local_experts, axis=1)
+    gated = jnp.where(takes, own_gates[:, :, None, :], 0.0)
+    slot_gate = jnp.sum(gated, axis=3)
+    arrived = jnp.einsum(
+        "sect,std->secd", one_hot, normed_all, preferred_element_type=jnp.float32
+    ).astype(jnp.bfloat16)
     gate_pre, up_pre, hidden = expert_forward(arrived, w_gate, w_up)
     result = jnp.einsum(
         "secf,efd->secd", hidden, w_down, preferred_element_type=jnp.float32
     ).astype(jnp.bfloat16)
-    returned = lax.all_to_all(
-        result.reshape(owner_count, local_experts * CAP, width),
+    expert_part = jnp.einsum(
+        "sect,secd->std", gated.astype(jnp.bfloat16), result, preferred_element_type=jnp.float32
+    ).astype(jnp.bfloat16)
+    expert_sum = lax.psum_scatter(
+        expert_part.reshape(owner_count * tok_rows, width),
         "expert",
-        split_axis=0,
-        concat_axis=0,
+        scatter_dimension=0,
         tiled=True,
     )
-    returned = returned.reshape(EXPERTS * CAP, width)
+    out_tokens = (residual + expert_sum.astype(jnp.float32)).astype(jnp.bfloat16)
     grad_flow = cotangent.astype(jnp.float32)
-    expert_sum = jnp.zeros((tok_rows, width), jnp.float32)
-    grad_list = []
-    for pick_index in range(TOP):
-        gathered = returned[slot_of[:, pick_index]].astype(jnp.float32)
-        expert_sum = expert_sum + gate_vals[:, pick_index : pick_index + 1] * gathered
-        grad_list.append(jnp.sum(grad_flow * gathered, axis=1))
-    out_tokens = (residual + expert_sum).astype(jnp.bfloat16)
-    grad_gates = jnp.stack(grad_list, axis=1)
-    grad_padded = jnp.concatenate([cotangent, jnp.zeros((1, width), jnp.bfloat16)], axis=0)
-    slot_grad = (grad_padded[slot_owner].astype(jnp.float32) * slot_gate[:, None]).astype(
-        jnp.bfloat16
-    )
-    slot_grad = slot_grad.reshape(owner_count, local_experts * CAP, width)
-    back_grad = lax.all_to_all(slot_grad, "expert", split_axis=0, concat_axis=0, tiled=True)
-    back_grad = back_grad.reshape(owner_count, local_experts, CAP, width)
-    grad_down = jnp.einsum("secf,secd->efd", hidden, back_grad, preferred_element_type=jnp.float32)
+    slot_dots = jnp.sum(grad_taken.astype(jnp.float32) * result.astype(jnp.float32), axis=3)
+    grad_gates = jnp.sum(jnp.where(takes, slot_dots[:, :, :, None], 0.0), axis=2)
+    grad_gates = lax.all_to_all(grad_gates, "expert", split_axis=0, concat_axis=0, tiled=True)
+    grad_gates = grad_gates.reshape(EXPERTS, tok_rows)
+    back_grad = (grad_taken.astype(jnp.float32) * slot_gate[:, :, :, None]).astype(jnp.bfloat16)
     grad_hidden = jnp.einsum(
         "secd,efd->secf", back_grad, w_down, preferred_element_type=jnp.float32
     )
@@ -191,10 +187,6 @@
         grad_hidden * up_pre * sigmoid_gate * (1.0 + gate_pre * (1.0 - sigmoid_gate))
     ).astype(jnp.bfloat16)
     grad_up_pre = (grad_hidden * gate_pre * sigmoid_gate).astype(jnp.bfloat16)
-    grad_gate = jnp.einsum(
-        "secd,secf->edf", arrived, grad_gate_pre, preferred_element_type=jnp.float32
-    )
-    grad_up = jnp.einsum("secd,secf->edf", arrived, grad_up_pre, preferred_element_type=jnp.float32)
     grad_slots = jnp.einsum(
         "secf,edf->secd", grad_gate_pre, w_gate, preferred_element_type=jnp.float32
     )
@@ -202,14 +194,20 @@
         grad_slots
         + jnp.einsum("secf,edf->secd", grad_up_pre, w_up, preferred_element_type=jnp.float32)
     ).astype(jnp.bfloat16)
-    grad_rows = lax.all_to_all(
-        grad_slots.reshape(owner_count, local_experts * CAP, width),
+    grad_part = jnp.einsum(
+        "sect,secd->std", one_hot, grad_slots, preferred_element_type=jnp.float32
+    ).astype(jnp.bfloat16)
+    grad_rows = lax.psum_scatter(
+        grad_part.reshape(owner_count * tok_rows, width),
         "expert",
-        split_axis=0,
-        concat_axis=0,
+        scatter_dimension=0,
         tiled=True,
     )
-    grad_rows = grad_rows.reshape(EXPERTS * CAP, width)
+    grad_down = jnp.einsum("secf,secd->efd", hidden, back_grad, preferred_element_type=jnp.float32)
+    grad_gate = jnp.einsum(
+        "secd,secf->edf", arrived, grad_gate_pre, preferred_element_type=jnp.float32
+    )
+    grad_up = jnp.einsum("secd,secf->edf", arrived, grad_up_pre, preferred_element_type=jnp.float32)
     grad_gate, grad_up, grad_down = (
         lax.psum_scatter(
             grad_gate.astype(jnp.bfloat16), "dp", scatter_dimension=1, tiled=True
@@ -221,22 +219,26 @@
             grad_down.astype(jnp.bfloat16), "dp", scatter_dimension=1, tiled=True
         ).astype(jnp.float32),
     )
-    grad_chosen = gate_vals * (grad_gates - jnp.sum(gate_vals * grad_gates, axis=1, keepdims=True))
-    grad_logits = jnp.sum(jnp.where(is_chosen, grad_chosen[:, :, None], 0.0), axis=1).astype(
-        jnp.bfloat16
-    )
+    gate_vals = lax.dynamic_index_in_dim(gates, owner, axis=0, keepdims=False)
+    grad_logits = (
+        gate_vals * (grad_gates - jnp.sum(gate_vals * grad_gates, axis=0, keepdims=True))
+    ).astype(jnp.bfloat16)
     grad_router = jnp.einsum(
-        "sd,se->de", normed_ffn, grad_logits, preferred_element_type=jnp.float32
+        "et,td->ed", grad_logits, normed_ffn, preferred_element_type=jnp.float32
     )
     grad_normed_ffn = jnp.einsum(
-        "se,de->sd", grad_logits, w_router, preferred_element_type=jnp.float32
-    )
-    for pick_index in range(TOP):
-        grad_normed_ffn = grad_normed_ffn + grad_rows[slot_of[:, pick_index]].astype(jnp.float32)
+        "et,de->td", grad_logits, w_router, preferred_element_type=jnp.float32
+    )
+    grad_normed_ffn = grad_normed_ffn + grad_rows.astype(jnp.float32)
     grad_norm_part, grad_gain_ffn = rms_back(residual, scale_ffn, gain_ffn, grad_normed_ffn)
     grad_residual = grad_flow + grad_norm_part
     grad_branch = grad_residual.astype(jnp.bfloat16)
     grad_w_out = jnp.einsum("se,sd->ed", attended, grad_branch, preferred_element_type=jnp.float32)
+    both = ("dp", "expert")
+    grad_w_out = lax.psum(grad_w_out.astype(jnp.bfloat16), both)
+    small = jnp.concatenate(
+        [grad_router, jnp.broadcast_to(grad_gain_ffn[None, :], (8, width))], axis=0
+    )
     grad_attended = jnp.einsum("sd,ed->se", grad_branch, w_out, preferred_element_type=jnp.float32)
     grad_attended = grad_attended.astype(jnp.bfloat16).reshape(
         tok_rows, group_count, group_size, HD
@@ -283,20 +285,23 @@
     )
     grad_input_part, grad_gain_attn = rms_back(inputs, scale_attn, gain_attn, grad_normed_attn)
     grad_tokens = (grad_residual + grad_input_part).astype(jnp.bfloat16)
-    grad_query, grad_key, grad_value, grad_w_out, grad_gain_attn, grad_gain_ffn, grad_router = (
-        lax.psum(
-            (
-                grad_query,
-                grad_key,
-                grad_value,
-                grad_w_out,
-                grad_gain_attn,
-                grad_gain_ffn,
-                grad_router,
-            ),
-            ("dp", "expert"),
-        )
-    )
+    small = lax.psum(small, both)
+    grad_router, grad_gain_ffn = small[:EXPERTS].T, small[EXPERTS]
+    late = jnp.concatenate(
+        [
+            grad_query,
+            jnp.concatenate([grad_key, grad_value], axis=1),
+            jnp.broadcast_to(grad_gain_attn[None, :], (16, width)),
+        ],
+        axis=0,
+    ).astype(jnp.bfloat16)
+    late, grad_w_out = lax.optimization_barrier((late, grad_w_out))
+    grad_w_out = grad_w_out.astype(jnp.float32)
+    late = lax.psum(late, both).astype(jnp.float32)
+    grad_query = late[:width]
+    grad_key = late[width : 2 * width, : grad_key.shape[1]]
+    grad_value = late[width : 2 * width, grad_key.shape[1] :]
+    grad_gain_attn = late[2 * width]
     return (
         out_tokens,
         grad_tokens,

time: 1850 us -> 1270 us (0.69)
  blocking collectives: 597 us -> 33.4 us
  local copies, waits for them, and re-layouts: 289 us -> 16.2 us
  waiting for transfers between devices: 644 us -> 853 us
  matrix products: 212 us -> 275 us
    all_to_all x2 -> x0, blocking collectives: 558 us -> none  [the longest x1 281 us: shards(): lax.all_to_all(outgoing, 'expert', split_axis=0, concat_axis=0, tiled=True)]
    all_to_all x2 -> x1, waiting for transfers between devices: 471 us -> 7.74 us  [shards(): lax.all_to_all(grad_gates, 'expert', split_axis=0, concat_axis=0, tiled=T...]
    reduce_scatter x0 -> x2, waiting for transfers between devices: none -> 270 us  [the longest x1 148 us: shards(): lax.psum_scatter(expert_part.reshape(owner_count * tok_rows, width), 'exp...]
    gather x18 -> x0, local copies, waits for them, and re-layouts: 209 us -> none  [the longest x8 77.7 us: shards(): gathered = returned[slot_of[:, pick_index]].astype(jnp.float32)]
    all_gather x0 -> x2, waiting for transfers between devices: none -> 154 us  [the longest x1 93.4 us: shards(): normed_all = lax.all_gather(normed_ffn, 'expert')]
    psum x1 -> x3, waiting for transfers between devices: 173 us -> 285 us  [the longest x1 143 us: shards(): late = lax.psum(late, both).astype(jnp.float32)]
    reduce_scatter x1, waiting for transfers between devices: 0.01 us -> 46 us  [shards(): lax.psum_scatter(grad_down.astype(jnp.bfloat16), 'dp', scatter_dimension=...]
    reduce_scatter x1, waiting for transfers between devices: 0.01 us -> 45 us  [shards(): lax.psum_scatter(grad_gate.astype(jnp.bfloat16), 'dp', scatter_dimension=...]
  transfers between devices with their start and end apart: 6 -> 11, of which waited for: 3 -> 11; matrix products, arithmetic and copies ran while one was open for 13% -> 17% of each run, Pallas kernels for 0% -> 0%
where the time goes in v1:
time: 1270 us; the launch traced here: 1260 us
  waiting for transfers between devices  853 us (67%)
  matrix products  275 us (22%)
  other arithmetic  59.9 us (5%)
  blocking collectives  33.4 us (3%)
  local copies, waits for them, and re-layouts  16.2 us (1%)
  between operations  15.3 us (1%)
    reduce_scatter x1, waiting for transfers between devices, shards(): lax.psum_scatter(expert_part.reshape(owner_count * tok_rows, width), 'exp...  148 us
    psum x1, waiting for transfers between devices, shards(): late = lax.psum(late, both).astype(jnp.float32)  143 us
    reduce_scatter x1, waiting for transfers between devices, shards(): lax.psum_scatter(grad_part.reshape(owner_count * tok_rows, width), 'exper...  122 us
    psum x1, waiting for transfers between devices, shards(): small = lax.psum(small, both)  121 us
    all_gather x1, waiting for transfers between devices, shards(): normed_all = lax.all_gather(normed_ffn, 'expert')  93.4 us
    all_gather x1, waiting for transfers between devices, shards(): cot_all = lax.all_gather(cotangent, 'expert')  60.9 us
    reduce_scatter x1, waiting for transfers between devices, shards(): lax.psum_scatter(grad_down.astype(jnp.bfloat16), 'dp', scatter_dimension=...  46 us
    reduce_scatter x1, waiting for transfers between devices, shards(): lax.psum_scatter(grad_gate.astype(jnp.bfloat16), 'dp', scatter_dimension=...  45 us
  transfers between devices with their start and end apart: 11, of which 11 were waited for; matrix products, arithmetic and copies ran while one was open for 17% of the time, Pallas kernels for 0%

profile of v1, /device:TPU:0, one launch (start us, length us, event | category | flops | bytes accessed | tf_op | source)
XLA Modules:
  0.0 1257.7 jit_solution(13931272961216623546)
XLA Ops:
  18.9 7.3 fusion.124
  26.3 8.3 fusion.6
  34.6 7.5 fusion.87
  46.9 33.4 %all-gather = s32[64,512]{1,0:T(8,128)S(1)} all-gather(s32[8,512]{1,0:T(8,128)S(1)} %bitcast.250), channel_id=2, replica_groups=mesh['dp'=4,'expert'=8] {'expert'}, dimensions={0}, use_global_device_ids=true | all-gather | bytes 147456 | tf_op jit(solution)/shard_map/all_gather | solution.py:95
  81.5 93.4 %all-gather.6.cloned.1.call-done = bf16[4096,1024]{1,0:T(8,128)(2,1)} async-done(((bf16[512,1024]{1,0:T(8,128)(2,1)}), bf16[4096,1024]{1,0:T(8,128)(2,1)}) %all-gather.6.cloned.1.call-update) | async-done | bytes 8388624 | tf_op jit(solution)/shard_map/all_gather | solution.py:136
  174.9 6.0 fusion.125
  181.8 13.9 %fusion.38 = bf16[8,4,192,1024]{3,2,1,0:T(8,128)(2,1)} fusion(bf16[8,512,1024,1]{2,1,3,0:T(8,128)(2,1)} %bitcast.225, s32[8,4,512]{2,1,0:T(4,128)S(1)} %copy.91), kind=kOutput, calls=%fused_computation.59 | convolution fusion | flops 6451888128 | bytes 21037056 | tf_op jit(solution)/shard_map/sect,std->secd/dot_general | solution.py:159
  195.7 12.3 fusion.28
  208.0 17.4 %fusion.16 = (bf16[8,4,192,512]{3,2,0,1:T(8,128)(2,1)}, f32[4,8,192,512]{3,2,1,0:T(8,128)}) fusion(f32[4,8,192,512]{3,2,1,0:T(8,128)} %fusion.28, bf16[4,1024,512]{2,1,0:T(8,128)(2,1)} %param.25, bf16[8,4,192,1024]{3,2,1,0:T(8,128)(2,1)} %fusion.38), kind=kOutput, calls=%fused_computation.31 | convolution fusion | flops 6461325312 | bytes 48234496 | tf_op jit(solution)/shard_map/secd,edf->secf/dot_general | solution.py:65
  225.3 13.9 %convert_bitcast_fusion = bf16[8,4,192,1024]{3,2,0,1:T(8,128)(2,1)} fusion(bf16[8,4,192,512]{3,2,0,1:T(8,128)(2,1)} %get-tuple-element.45, bf16[4,512,1024]{2,1,0:T(8,128)(2,1)} %param.26), kind=kOutput, calls=%fused_computation.42 | convolution fusion | flops 6448742400 | bytes 23068672 | tf_op jit(solution)/shard_map/secf,efd->secd/dot_general | solution.py:163
  239.2 60.9 %all-gather.8.cloned.1.call-done = bf16[4096,1024]{1,0:T(8,128)(2,1)} async-done(((bf16[512,1024]{1,0:T(8,128)(2,1)}), bf16[4096,1024]{1,0:T(8,128)(2,1)}) %all-gather.8.cloned.1.call-update) | async-done | bytes 8388624 | tf_op jit(solution)/shard_map/all_gather | solution.py:94
  300.2 15.2 %fusion.1 = (f32[8,4,192]{2,0,1:T(8,128)S(1)}, bf16[8,4,192,1024]{3,2,0,1:T(8,128)(2,1)}) fusion(bf16[8,4,192,1024]{3,2,0,1:T(8,128)(2,1)} %convert_bitcast_fusion, bf16[8,512,1024,1]{2,1,0,3:T(8,128)(2,1)} %bitcast.256, s32[8,4,512]{2,1,0:T(4,128)S(1)} %copy.91), kind=kOutput, calls=%fused_computation.3 | convolution fusion | flops 6477047808 | bytes 33644544 | tf_op jit(solution)/shard_map/sect,std->secd/dot_general | solution.py:148
  315.4 5.4 select_reduce_fusion.1
  320.8 23.0 %fusion.15 = (bf16[8,4,192,512]{3,2,0,1:T(8,128)(2,1)}, bf16[8,4,192,512]{3,2,0,1:T(8,128)(2,1)}) fusion(f32[4,8,192,512]{3,2,1,0:T(8,128)} %fusion.28, f32[4,8,192,512]{3,2,1,0:T(8,128)} %get-tuple-element.46, bf16[4,512,1024]{2,1,0:T(8,128)(2,1)} %param.26, bf16[8,4,192,1024]{3,2,0,1:T(8,128)(2,1)} %get-tuple-element.48, f32[8,4,192]{2,0,1:T(8,128)S(1)} %copy.97), kind=kOutput, calls=%fused_computation.29 | convolution fusion | flops 6502219776 | bytes 54550528 | tf_op jit(solution)/shard_map/secd,efd->secf/dot_general | solution.py:182
  343.9 15.3 %fusion.59 = f32[4,8,192,1024]{3,2,0,1:T(8,128)} fusion(bf16[8,4,192,512]{3,2,0,1:T(8,128)(2,1)} %get-tuple-element.25, bf16[4,1024,512]{2,1,0:T(8,128)(2,1)} %param.24), kind=kOutput, calls=%fused_computation.72 | convolution fusion | flops 6442450944 | bytes 35651584 | tf_op jit(solution)/shard_map/secf,edf->secd/dot_general | solution.py:190
  359.2 22.2 %bitcast_convert_fusion = bf16[8,512,1024]{2,1,0:T(8,128)(2,1)} fusion(f32[4,8,192,1024]{3,2,0,1:T(8,128)} %fusion.59, s32[8,4,512]{2,1,0:T(4,128)S(1)} %copy.91, bf16[8,4,192,512]{3,2,0,1:T(8,128)(2,1)} %get-tuple-element.24, bf16[4,1024,512]{2,1,0:T(8,128)(2,1)} %param.25), kind=kOutput, calls=%fused_computation.11 | convolution fusion | flops 12904824832 | bytes 44105728 | tf_op jit(solution)/shard_map/sect,secd->std/dot_general | solution.py:197
  381.5 13.6 %bitcast_convert_fusion.1 = bf16[8,512,1024]{2,1,0:T(8,128)(2,1)} fusion(bf16[8,4,192,1024]{3,2,0,1:T(8,128)(2,1)} %convert_bitcast_fusion, f32[8,4,512]{2,1,0:T(4,128)S(1)} %constant_dynamic-slice_fusion, s32[8,4,512]{2,1,0:T(4,128)S(1)} %copy.91), kind=kOutput, calls=%fused_computation.12 | convolution fusion | flops 6452936704 | bytes 21102592 | tf_op jit(solution)/shard_map/sect,secd->std/dot_general | solution.py:166
  398.8 7.7 all-to-all-done
  408.3 121.8 %reduce-scatter.8.cloned.1.call-done = bf16[512,1024]{1,0:T(8,128)(2,1)} async-done(((bf16[4096,1024]{1,0:T(8,128)(2,1)}), bf16[512,1024]{1,0:T(8,128)(2,1)}) %reduce-scatter.8.cloned.1.call-update) | async-done | bytes 1048592 | tf_op jit(solution)/shard_map/reduce_scatter | solution.py:200
  534.1 148.0 %reduce-scatter.6.cloned.1.call-done = bf16[512,1024]{1,0:T(8,128)(2,1)} async-done(((bf16[4096,1024]{1,0:T(8,128)(2,1)}), bf16[512,1024]{1,0:T(8,128)(2,1)}) %reduce-scatter.6.cloned.1.call-update) | async-done | bytes 1048592 | tf_op jit(solution)/shard_map/reduce_scatter | solution.py:169
  690.3 12.3 bitcast_convert_fusion.2
  702.7 13.0 %bitcast_convert_fusion.3 = bf16[4,1024,512]{2,1,0:T(8,128)(2,1)} fusion(bf16[8,4,192,1024]{3,2,1,0:T(8,128)(2,1)} %fusion.38, bf16[8,4,192,512]{3,2,0,1:T(8,128)(2,1)} %get-tuple-element.24), kind=kOutput, calls=%fused_computation.55 | convolution fusion | flops 6444548096 | bytes 23068672 | tf_op jit(solution)/shard_map/secd,secf->edf/dot_general | solution.py:210
  715.8 13.1 %bitcast_convert_fusion.4 = bf16[4,1024,512]{2,1,0:T(8,128)(2,1)} fusion(bf16[8,4,192,1024]{3,2,1,0:T(8,128)(2,1)} %fusion.38, bf16[8,4,192,512]{3,2,0,1:T(8,128)(2,1)} %get-tuple-element.25), kind=kOutput, calls=%fused_computation.56 | convolution fusion | flops 6444548096 | bytes 23068672 | tf_op jit(solution)/shard_map/secd,secf->edf/dot_general | solution.py:207
  734.4 15.9 %fusion.3 = (f32[8,2,512]{2,1,0:T(2,128)S(1)}, f32[8,512,512,2]{2,1,3,0:T(8,128)}) fusion(f32[8,2,512,512]{2,3,1,0:T(8,128)} %get-tuple-element.42, f32[8,2,512]{2,1,0:T(2,128)S(1)} %bitcast.245, bf16[512,8,64,1]{0,2,3,1:T(8,128)(2,1)} %bitcast.243, bf16[512,8,2,64]{0,3,2,1:T(8,128)(2,1)} %bitcast.221), kind=kOutput, calls=%fused_computation.8 | convolution fusion | flops 549445632 | bytes 35192832 | tf_op jit(solution)/shard_map/qgrd,kgd->grqk/dot_general | solution.py:247
  750.3 11.0 fusion.5
  761.4 6.1 fusion.92
  802.5 20.6 %all-reduce.4.cloned.1.call-done = bf16[1024,1024]{1,0:T(8,128)(2,1)} async-done(((bf16[1024,1024]{1,0:T(8,128)(2,1)}), bf16[1024,1024]{1,0:T(8,128)(2,1)}) %all-reduce.4.cloned.1.call-update) | async-done | bytes 2097168 | tf_op jit(solution)/shard_map/psum | solution.py:238
  823.2 46.0 %reduce-scatter.14.cloned.1.call-done = bf16[4,128,1024]{2,1,0:T(8,128)(2,1)} async-done(((bf16[4,512,1024]{2,1,0:T(8,128)(2,1)}), bf16[4,128,1024]{2,1,0:T(8,128)(2,1)}) %reduce-scatter.14.cloned.1.call-update) | async-done | bytes 1048592 | tf_op jit(solution)/shard_map/reduce_scatter | solution.py:218
  871.9 44.8 %reduce-scatter.12.cloned.1.call-done = bf16[4,256,512]{2,1,0:T(8,128)(2,1)} async-done(((bf16[4,1024,512]{2,1,0:T(8,128)(2,1)}), bf16[4,256,512]{2,1,0:T(8,128)(2,1)}) %reduce-scatter.12.cloned.1.call-update) | async-done | bytes 1048592 | tf_op jit(solution)/shard_map/reduce_scatter | solution.py:215
  919.6 45.0 %reduce-scatter.10.cloned.1.call-done = bf16[4,256,512]{2,1,0:T(8,128)(2,1)} async-done(((bf16[4,1024,512]{2,1,0:T(8,128)(2,1)}), bf16[4,256,512]{2,1,0:T(8,128)(2,1)}) %reduce-scatter.10.cloned.1.call-update) | async-done | bytes 1048592 | tf_op jit(solution)/shard_map/reduce_scatter | solution.py:212
  971.2 120.9 %all-reduce.8.cloned.1.call-done = f32[40,1024]{1,0:T(8,128)} async-done(((f32[40,1024]{1,0:T(8,128)}), f32[40,1024]{1,0:T(8,128)}) %all-reduce.8.cloned.1.call-update) | async-done | bytes 163856 | tf_op jit(solution)/shard_map/psum | solution.py:288
  1099.0 143.2 %all-reduce.6.cloned.1.call-done = bf16[2064,1024]{1,0:T(8,128)(2,1)} async-done(((bf16[2064,1024]{1,0:T(8,128)(2,1)}), bf16[2064,1024]{1,0:T(8,128)(2,1)}) %all-reduce.6.cloned.1.call-update) | async-done | bytes 4227088 | tf_op jit(solution)/shard_map/psum | solution.py:300
  (189 shorter events, 103.9 us)
Async XLA Ops:
  7.2 35.0 %copy-start = (bf16[1024,1024]{1,0:T(8,128)(2,1)S(1)}, bf16[1024,1024]{1,0:T(8,128)(2,1)}, u32[]{:S(2)}) copy-start(bf16[1024,1024]{1,0:T(8,128)(2,1)} %param.21) | copy-start | bytes 6291460
  7.2 8.7 copy-start.2
  7.2 8.7 copy-start.40
  7.2 167.7 %all-gather.6.cloned.1.call-start = ((), (), s32[]{:S(2)}) async-start(), calls=%async_computation.14 | async-start | bytes 9437184 | tf_op jit(solution)/shard_map/all_gather | solution.py:136
  13.3 21.2 %copy-start.27 = (bf16[512,512]{0,1:T(8,128)(2,1)}, bf16[512,512]{0,1:T(8,128)(2,1)S(1)}, u32[]{:S(2)}) copy-start(bf16[512,512]{0,1:T(8,128)(2,1)S(1)} %convolution_convert_fusion.5) | copy-start | bytes 1572868
  42.1 132.8 %copy-start.28 = (bf16[1024,32]{0,1:T(8,128)(2,1)S(1)}, bf16[1024,32]{0,1:T(8,128)(2,1)}, u32[]{:S(2)}) copy-start(bf16[1024,32]{0,1:T(8,128)(2,1)} %param.23) | copy-start | bytes 196612
  46.1 254.1 %all-gather.8.cloned.1.call-start = ((), (), s32[]{:S(2)}) async-start(), calls=%async_computation.15 | async-start | bytes 9437184 | tf_op jit(solution)/shard_map/all_gather | solution.py:94
  46.9 483.3 %reduce-scatter.8.cloned.1.call-start = ((), (), s32[]{:S(2)}) async-start(), calls=%async_computation.7 | async-start | bytes 9437184 | tf_op jit(solution)/shard_map/reduce_scatter | solution.py:200
  181.8 13.9 %copy-start.43 = (bf16[4,1024,512]{2,1,0:T(8,128)(2,1)S(1)}, bf16[4,1024,512]{2,1,0:T(8,128)(2,1)}, u32[]{:S(2)}) copy-start(bf16[4,1024,512]{2,1,0:T(8,128)(2,1)} %param.24) | copy-start | bytes 12582916
  381.4 300.7 %reduce-scatter.6.cloned.1.call-start = ((), (), s32[]{:S(2)}) async-start(), calls=%async_computation.6 | async-start | bytes 9437184 | tf_op jit(solution)/shard_map/reduce_scatter | solution.py:169
  395.1 135.0 %copy-start.29 = (bf16[1024,32]{0,1:T(8,128)(2,1)S(1)}, bf16[1024,32]{0,1:T(8,128)(2,1)}, u32[]{:S(2)}) copy-start(bf16[1024,32]{0,1:T(8,128)(2,1)} %param.23) | copy-start | bytes 196612
  395.1 135.0 %copy-start.35 = (f32[1024]{0:T(1024)S(1)}, f32[1024]{0:T(1024)}, u32[]{:S(2)}) copy-start(f32[1024]{0:T(1024)} %param.22) | copy-start | bytes 12292
  395.1 135.0 %copy-start.37 = (f32[512]{0:T(512)S(1)}, f32[512]{0:T(512)}, u32[]{:S(2)}) copy-start(f32[512]{0:T(512)} %copy-done.36) | copy-start | bytes 6148
  395.1 287.0 %copy-start.6 = (bf16[512,1024]{1,0:T(8,128)(2,1)S(1)}, bf16[512,1024]{1,0:T(8,128)(2,1)}, u32[]{:S(2)}) copy-start(bf16[512,1024]{1,0:T(8,128)(2,1)} %param.27) | copy-start | bytes 3145732
  395.1 11.5 all-to-all-start
  398.6 424.5 %all-reduce.4.cloned.1.call-start = ((), (), s32[]{:S(2)}) async-start(), calls=%async_computation.8 | async-start | bytes 4194304 | tf_op jit(solution)/shard_map/psum | solution.py:238
  690.3 178.9 %reduce-scatter.14.cloned.1.call-start = ((), (), s32[]{:S(2)}) async-start(), calls=%async_computation.13 | async-start | bytes 5242880 | tf_op jit(solution)/shard_map/reduce_scatter | solution.py:218
  702.6 214.1 %reduce-scatter.12.cloned.1.call-start = ((), (), s32[]{:S(2)}) async-start(), calls=%async_computation.12 | async-start | bytes 5242880 | tf_op jit(solution)/shard_map/reduce_scatter | solution.py:215
  715.7 13.5 %copy-start.31 = (f32[8,2,512]{2,1,0:T(2,128)S(1)}, f32[8,2,512]{2,1,0:T(2,128)}, u32[]{:S(2)}) copy-start(f32[8,2,512]{2,1,0:T(2,128)} %copy-done.30) | copy-start | bytes 98308
  715.7 13.5 %copy-start.33 = (f32[8,2,512]{2,1,0:T(2,128)S(1)}, f32[8,2,512]{2,1,0:T(2,128)}, u32[]{:S(2)}) copy-start(f32[8,2,512]{2,1,0:T(2,128)} %copy-done.32) | copy-start | bytes 98308
  715.7 13.5 %copy-start.4 = (bf16[512,1024]{1,0:T(8,128)(2,1)S(1)}, bf16[512,1024]{1,0:T(8,128)(2,1)}, u32[]{:S(2)}) copy-start(bf16[512,1024]{1,0:T(8,128)(2,1)} %multiply_convert_fusion) | copy-start | bytes 3145732
  715.7 248.8 %reduce-scatter.10.cloned.1.call-start = ((), (), s32[]{:S(2)}) async-start(), calls=%async_computation.11 | async-start | bytes 5242880 | tf_op jit(solution)/shard_map/reduce_scatter | solution.py:212
  728.9 363.2 %all-reduce.8.cloned.1.call-start = ((), (), s32[]{:S(2)}) async-start(), calls=%async_computation.10 | async-start | bytes 327680 | tf_op jit(solution)/shard_map/psum | solution.py:288
  734.4 15.9 %slice-start = ((s8[16777216]{0:T(1024)(128)(4,1)}), s8[4194304]{0:T(1024)(128)(4,1)S(1)}, s32[]{:S(2)}) async-start(s8[16777216]{0:T(1024)(128)(4,1)} %bitcast.217), calls=%async_computation.16 | async-start | bytes 8388608
  734.4 15.9 %slice-start.1 = ((s8[16777216]{0:T(1024)(128)(4,1)}), s8[4194304]{0:T(1024)(128)(4,1)S(1)}, s32[]{:S(2)}) async-start(s8[16777216]{0:T(1024)(128)(4,1)} %bitcast.217), calls=%async_computation.17 | async-start | bytes 8388608
  734.4 15.9 %slice-start.2 = ((s8[16777216]{0:T(1024)(128)(4,1)}), s8[4194304]{0:T(1024)(128)(4,1)S(1)}, s32[]{:S(2)}) async-start(s8[16777216]{0:T(1024)(128)(4,1)} %bitcast.217), calls=%async_computation.18 | async-start | bytes 8388608
  734.4 15.9 %slice-start.3 = ((s8[16777216]{0:T(1024)(128)(4,1)}), s8[4194304]{0:T(1024)(128)(4,1)S(1)}, s32[]{:S(2)}) async-start(s8[16777216]{0:T(1024)(128)(4,1)} %bitcast.217), calls=%async_computation.19 | async-start | bytes 8388608
  750.3 11.0 copy-start.8
  750.3 11.0 copy-start.10
  779.9 9.0 copy-start.3
  779.9 8.9 copy-start.16
  794.3 448.0 %all-reduce.6.cloned.1.call-start = ((), (), s32[]{:S(2)}) async-start(), calls=%async_computation.9 | async-start | bytes 8454144 | tf_op jit(solution)/shard_map/psum | solution.py:300
  (31 other events, 165.2 us)
Sparse Core Ops, SparseCore 0:
  46.2 128.6 all-gather.5
  177.0 123.1 all-gather.7
  381.6 148.5 reduce-scatter.7
  534.0 147.9 reduce-scatter.5
  690.4 132.7 all-reduce.3
  825.7 43.3 reduce-scatter.13
  872.2 44.4 reduce-scatter.11
  920.0 44.4 reduce-scatter.9
  970.1 121.8 all-reduce.7
  1097.6 144.6 all-reduce.5

commit v2 on v1

--- a/solution.py
+++ b/solution.py
@@ -133,7 +133,8 @@
     residual = inputs + jnp.dot(attended, w_out, preferred_element_type=jnp.float32)
     scale_ffn = rms_scale(residual)
     normed_ffn = (residual * scale_ffn * gain_ffn).astype(jnp.bfloat16)
-    normed_all = lax.all_gather(normed_ffn, "expert")
+    sent_rows, cot_all = lax.optimization_barrier((normed_ffn, cot_all))
+    normed_all = lax.all_gather(sent_rows, "expert")
     earlier = (places[:, None] < places[None, :]).astype(jnp.bfloat16)
     expert_ids = jnp.arange(EXPERTS, dtype=jnp.int32)
     chosen = jnp.any(picks_all[:, :, None, :] == expert_ids[None, None, :, None], axis=1)
@@ -166,6 +167,7 @@
     expert_part = jnp.einsum(
         "sect,secd->std", gated.astype(jnp.bfloat16), result, preferred_element_type=jnp.float32
     ).astype(jnp.bfloat16)
+    expert_part, grad_taken = lax.optimization_barrier((expert_part, grad_taken))
     expert_sum = lax.psum_scatter(
         expert_part.reshape(owner_count * tok_rows, width),
         "expert",
@@ -209,14 +211,18 @@
     )
     grad_up = jnp.einsum("secd,secf->edf", arrived, grad_up_pre, preferred_element_type=jnp.float32)
     grad_gate, grad_up, grad_down = (
+        item.astype(jnp.bfloat16) for item in (grad_gate, grad_up, grad_down)
+    )
+    grad_rows = lax.optimization_barrier((grad_rows, grad_gate, grad_up, grad_down))[0]
+    grad_gate, grad_up, grad_down = (
         lax.psum_scatter(
-            grad_gate.astype(jnp.bfloat16), "dp", scatter_dimension=1, tiled=True
+            grad_gate, "dp", scatter_dimension=1, tiled=True
         ).astype(jnp.float32),
         lax.psum_scatter(
-            grad_up.astype(jnp.bfloat16), "dp", scatter_dimension=1, tiled=True
+            grad_up, "dp", scatter_dimension=1, tiled=True
         ).astype(jnp.float32),
         lax.psum_scatter(
-            grad_down.astype(jnp.bfloat16), "dp", scatter_dimension=1, tiled=True
+            grad_down, "dp", scatter_dimension=1, tiled=True
         ).astype(jnp.float32),
     )
     gate_vals = lax.dynamic_index_in_dim(gates, owner, axis=0, keepdims=False)
@@ -224,7 +230,7 @@
         gate_vals * (grad_gates - jnp.sum(gate_vals * grad_gates, axis=0, keepdims=True))
     ).astype(jnp.bfloat16)
     grad_router = jnp.einsum(
-        "et,td->ed", grad_logits, normed_ffn, preferred_element_type=jnp.float32
+        "et,td->de", grad_logits, normed_ffn, preferred_element_type=jnp.float32
     )
     grad_normed_ffn = jnp.einsum(
         "et,de->td", grad_logits, w_router, preferred_element_type=jnp.float32
@@ -234,11 +240,6 @@
     grad_residual = grad_flow + grad_norm_part
     grad_branch = grad_residual.astype(jnp.bfloat16)
     grad_w_out = jnp.einsum("se,sd->ed", attended, grad_branch, preferred_element_type=jnp.float32)
-    both = ("dp", "expert")
-    grad_w_out = lax.psum(grad_w_out.astype(jnp.bfloat16), both)
-    small = jnp.concatenate(
-        [grad_router, jnp.broadcast_to(grad_gain_ffn[None, :], (8, width))], axis=0
-    )
     grad_attended = jnp.einsum("sd,ed->se", grad_branch, w_out, preferred_element_type=jnp.float32)
     grad_attended = grad_attended.astype(jnp.bfloat16).reshape(
         tok_rows, group_count, group_size, HD
@@ -285,23 +286,25 @@
     )
     grad_input_part, grad_gain_attn = rms_back(inputs, scale_attn, gain_attn, grad_normed_attn)
     grad_tokens = (grad_residual + grad_input_part).astype(jnp.bfloat16)
-    small = lax.psum(small, both)
-    grad_router, grad_gain_ffn = small[:EXPERTS].T, small[EXPERTS]
-    late = jnp.concatenate(
+    small = jnp.concatenate(
         [
-            grad_query,
-            jnp.concatenate([grad_key, grad_value], axis=1),
-            jnp.broadcast_to(grad_gain_attn[None, :], (16, width)),
+            grad_router,
+            grad_gain_attn[:, None],
+            grad_gain_ffn[:, None],
+            jnp.zeros((width, 128 - EXPERTS - 2), jnp.float32),
         ],
-        axis=0,
-    ).astype(jnp.bfloat16)
-    late, grad_w_out = lax.optimization_barrier((late, grad_w_out))
-    grad_w_out = grad_w_out.astype(jnp.float32)
-    late = lax.psum(late, both).astype(jnp.float32)
-    grad_query = late[:width]
-    grad_key = late[width : 2 * width, : grad_key.shape[1]]
-    grad_value = late[width : 2 * width, grad_key.shape[1] :]
-    grad_gain_attn = late[2 * width]
+        axis=1,
+    )
+    sums = [
+        item.astype(jnp.bfloat16)
+        for item in (grad_query, grad_key, grad_value, grad_w_out, small)
+    ]
+    sums = lax.psum(tuple(lax.optimization_barrier(sums)), ("dp", "expert"))
+    grad_query, grad_key, grad_value, grad_w_out, small = (
+        item.astype(jnp.float32) for item in sums
+    )
+    grad_router = small[:, :EXPERTS]
+    grad_gain_attn, grad_gain_ffn = small[:, EXPERTS], small[:, EXPERTS + 1]
     return (
         out_tokens,
         grad_tokens,

time: 1270 us -> 1060 us (0.83)
  waiting for transfers between devices: 853 us -> 648 us
    psum x3 -> x1, waiting for transfers between devices: 285 us -> 162 us  [shards(): sums = lax.psum(tuple(lax.optimization_barrier(sums)), ('dp', 'expert'))]
    reduce_scatter x3, waiting for transfers between devices: 136 us -> 60.3 us  [the longest x1 44.8 us: shards(): lax.psum_scatter(grad_gate, 'dp', scatter_dimension=1, tiled=True)]
    all_gather x1, waiting for transfers between devices: 60.9 us -> 92.3 us  [shards(): cot_all = lax.all_gather(cotangent, 'expert')]
    reduce_scatter x1, waiting for transfers between devices: 122 us -> 104 us  [shards(): lax.psum_scatter(grad_part.reshape(owner_count * tok_rows, width), 'exper...]
  transfers between devices with their start and end apart: 11 -> 9, of which waited for: 11 -> 7; matrix products, arithmetic and copies ran while one was open for 17% -> 17% of each run, Pallas kernels for 0% -> 0%
where the time goes in v2:
time: 1060 us; the launch traced here: 1050 us
  waiting for transfers between devices  648 us (61%)
  matrix products  268 us (25%)
  other arithmetic  70.5 us (7%)
  blocking collectives  31.4 us (3%)
  between operations  15.4 us (1%)
    psum x1, waiting for transfers between devices, shards(): sums = lax.psum(tuple(lax.optimization_barrier(sums)), ('dp', 'expert'))  162 us
    reduce_scatter x1, waiting for transfers between devices, shards(): lax.psum_scatter(expert_part.reshape(owner_count * tok_rows, width), 'exp...  148 us
    reduce_scatter x1, waiting for transfers between devices, shards(): lax.psum_scatter(grad_part.reshape(owner_count * tok_rows, width), 'exper...  104 us
    all_gather x1, waiting for transfers between devices, shards(): cot_all = lax.all_gather(cotangent, 'expert')  92.3 us
    all_gather x1, waiting for transfers between devices, shards(): normed_all = lax.all_gather(sent_rows, 'expert')  80.7 us
    reduce_scatter x1, waiting for transfers between devices, shards(): lax.psum_scatter(grad_gate, 'dp', scatter_dimension=1, tiled=True)  44.8 us
    all_gather x1, blocking collectives, shards(): picks_all = lax.all_gather(expert_picks.T, 'expert')  31.4 us
    dot_general x1, matrix products, shards(): jnp.einsum('secd,efd->secf', back_grad, w_down, preferred_element_type=jn...  23.4 us
  transfers between devices with their start and end apart: 9, of which 7 were waited for; matrix products, arithmetic and copies ran while one was open for 17% of the time, Pallas kernels for 0%

profile of v2, /device:TPU:0, one launch (start us, length us, event | category | flops | bytes accessed | tf_op | source)
XLA Modules:
  0.0 1045.7 jit_solution(5199545634476171293)
XLA Ops:
  17.8 7.8 fusion.127
  25.6 8.3 fusion.6
  34.0 7.6 fusion.90
  45.6 92.3 %all-gather.6.cloned.1.call-done = bf16[4096,1024]{1,0:T(8,128)(2,1)} async-done(((bf16[512,1024]{1,0:T(8,128)(2,1)}), bf16[4096,1024]{1,0:T(8,128)(2,1)}) %all-gather.6.cloned.1.call-update) | async-done | bytes 8388624 | tf_op jit(solution)/shard_map/all_gather | solution.py:94
  137.9 31.4 %all-gather = s32[64,512]{1,0:T(8,128)S(1)} all-gather(s32[8,512]{1,0:T(8,128)S(1)} %bitcast.248), channel_id=2, replica_groups=mesh['dp'=4,'expert'=8] {'expert'}, dimensions={0}, use_global_device_ids=true | all-gather | bytes 147456 | tf_op jit(solution)/shard_map/all_gather | solution.py:95
  170.5 13.1 %fusion.40 = bf16[8,4,192,1024]{3,2,0,1:T(8,128)(2,1)} fusion(bf16[8,512,1024]{2,1,0:T(8,128)(2,1)} %bitcast.254, s32[8,4,512]{2,1,0:T(4,128)S(1)} %copy.85), kind=kOutput, calls=%fused_computation.61 | convolution fusion | flops 6451888128 | bytes 21037056 | tf_op jit(solution)/shard_map/sect,std->secd/dot_general | solution.py:149
  183.5 80.7 %all-gather.8.cloned.1.call-done = bf16[4096,1024]{1,0:T(8,128)(2,1)} async-done(((bf16[512,1024]{1,0:T(8,128)(2,1)}), bf16[4096,1024]{1,0:T(8,128)(2,1)}) %all-gather.8.cloned.1.call-update) | async-done | bytes 8388624 | tf_op jit(solution)/shard_map/all_gather | solution.py:137
  264.3 6.0 fusion.128
  271.2 13.1 %fusion.39 = bf16[8,4,192,1024]{3,2,1,0:T(8,128)(2,1)} fusion(bf16[8,512,1024,1]{2,1,3,0:T(8,128)(2,1)} %bitcast.224, s32[8,4,512]{2,1,0:T(4,128)S(1)} %copy.85), kind=kOutput, calls=%fused_computation.60 | convolution fusion | flops 6451888128 | bytes 21037056 | tf_op jit(solution)/shard_map/sect,std->secd/dot_general | solution.py:160
  284.3 12.3 %fusion.28 = f32[4,8,192,512]{3,2,1,0:T(8,128)} fusion(bf16[8,4,192,1024]{3,2,1,0:T(8,128)(2,1)} %fusion.39, bf16[4,1024,512]{2,1,0:T(8,128)(2,1)S(1)} %copy-done.47), kind=kOutput, calls=%fused_computation.49 | convolution fusion | flops 6442450944 | bytes 29360128 | tf_op jit(solution)/shard_map/secd,edf->secf/dot_general | solution.py:64
  296.6 17.5 %fusion.16 = (bf16[8,4,192,512]{3,2,0,1:T(8,128)(2,1)}, f32[4,8,192,512]{3,2,1,0:T(8,128)}) fusion(f32[4,8,192,512]{3,2,1,0:T(8,128)} %fusion.28, bf16[4,1024,512]{2,1,0:T(8,128)(2,1)} %param.25, bf16[8,4,192,1024]{3,2,1,0:T(8,128)(2,1)} %fusion.39), kind=kOutput, calls=%fused_computation.31 | convolution fusion | flops 6461325312 | bytes 48234496 | tf_op jit(solution)/shard_map/secd,edf->secf/dot_general | solution.py:65
  314.1 12.7 %convert_bitcast_fusion = bf16[8,4,192,1024]{3,2,0,1:T(8,128)(2,1)} fusion(bf16[8,4,192,512]{3,2,0,1:T(8,128)(2,1)} %get-tuple-element.66, bf16[4,512,1024]{2,1,0:T(8,128)(2,1)} %param.26), kind=kOutput, calls=%fused_computation.42 | convolution fusion | flops 6448742400 | bytes 23068672 | tf_op jit(solution)/shard_map/secf,efd->secd/dot_general | solution.py:164
  326.7 13.6 %bitcast_convert_fusion.1 = bf16[8,512,1024]{2,1,0:T(8,128)(2,1)} fusion(bf16[8,4,192,1024]{3,2,0,1:T(8,128)(2,1)} %convert_bitcast_fusion, f32[8,4,512]{2,1,0:T(4,128)S(1)} %constant_dynamic-slice_fusion, s32[8,4,512]{2,1,0:T(4,128)S(1)} %copy.85), kind=kOutput, calls=%fused_computation.12 | convolution fusion | flops 6452936704 | bytes 21102592 | tf_op jit(solution)/shard_map/sect,secd->std/dot_general | solution.py:167
  340.3 9.0 fusion.1
  349.3 5.4 select_reduce_fusion.1
  354.7 23.4 %fusion.15 = (bf16[8,4,192,512]{3,2,0,1:T(8,128)(2,1)}, bf16[8,4,192,512]{3,2,0,1:T(8,128)(2,1)}) fusion(f32[4,8,192,512]{3,2,1,0:T(8,128)} %fusion.28, f32[4,8,192,512]{3,2,1,0:T(8,128)} %get-tuple-element.67, bf16[4,512,1024]{2,1,0:T(8,128)(2,1)} %param.26, bf16[8,4,192,1024]{3,2,0,1:T(8,128)(2,1)} %fusion.40, f32[8,4,192]{2,0,1:T(8,128)S(1)} %copy.91), kind=kOutput, calls=%fused_computation.29 | convolution fusion | flops 6502219776 | bytes 54550528 | tf_op jit(solution)/shard_map/secd,efd->secf/dot_general | solution.py:184
  378.1 14.9 %fusion.62 = f32[4,8,192,1024]{3,2,0,1:T(8,128)} fusion(bf16[8,4,192,512]{3,2,0,1:T(8,128)(2,1)} %get-tuple-element.46, bf16[4,1024,512]{2,1,0:T(8,128)(2,1)} %param.24), kind=kOutput, calls=%fused_computation.73 | convolution fusion | flops 6442450944 | bytes 35651584 | tf_op jit(solution)/shard_map/secf,edf->secd/dot_general | solution.py:192
  393.1 22.3 %bitcast_convert_fusion = bf16[8,512,1024]{2,1,0:T(8,128)(2,1)} fusion(f32[4,8,192,1024]{3,2,0,1:T(8,128)} %fusion.62, s32[8,4,512]{2,1,0:T(4,128)S(1)} %copy.85, bf16[8,4,192,512]{3,2,0,1:T(8,128)(2,1)} %get-tuple-element.45, bf16[4,1024,512]{2,1,0:T(8,128)(2,1)} %param.25), kind=kOutput, calls=%fused_computation.11 | convolution fusion | flops 12904824832 | bytes 44105728 | tf_op jit(solution)/shard_map/sect,secd->std/dot_general | solution.py:199
  416.0 12.5 %bitcast_convert_fusion.2 = bf16[4,512,1024]{2,1,0:T(8,128)(2,1)} fusion(bf16[8,4,192,512]{3,2,0,1:T(8,128)(2,1)} %get-tuple-element.66, bf16[8,4,192,1024]{3,2,0,1:T(8,128)(2,1)} %fusion.40, f32[8,4,192]{2,0,1:T(8,128)S(1)} %copy.91), kind=kOutput, calls=%fused_computation.54 | convolution fusion | flops 6463422464 | bytes 23093248 | tf_op jit(solution)/shard_map/secf,secd->efd/dot_general | solution.py:208
  428.6 12.9 %bitcast_convert_fusion.3 = bf16[4,1024,512]{2,1,0:T(8,128)(2,1)} fusion(bf16[8,4,192,1024]{3,2,1,0:T(8,128)(2,1)} %fusion.39, bf16[8,4,192,512]{3,2,0,1:T(8,128)(2,1)} %get-tuple-element.45), kind=kOutput, calls=%fused_computation.55 | convolution fusion | flops 6444548096 | bytes 23068672 | tf_op jit(solution)/shard_map/secd,secf->edf/dot_general | solution.py:212
  445.1 13.0 %bitcast_convert_fusion.4 = bf16[4,1024,512]{2,1,0:T(8,128)(2,1)} fusion(bf16[8,4,192,1024]{3,2,1,0:T(8,128)(2,1)} %fusion.39, bf16[8,4,192,512]{3,2,0,1:T(8,128)(2,1)} %get-tuple-element.46), kind=kOutput, calls=%fused_computation.56 | convolution fusion | flops 6444548096 | bytes 23068672 | tf_op jit(solution)/shard_map/secd,secf->edf/dot_general | solution.py:209
  460.2 103.8 %reduce-scatter.8.cloned.1.call-done = bf16[512,1024]{1,0:T(8,128)(2,1)} async-done(((bf16[4096,1024]{1,0:T(8,128)(2,1)}), bf16[512,1024]{1,0:T(8,128)(2,1)}) %reduce-scatter.8.cloned.1.call-update) | async-done | bytes 1048592 | tf_op jit(solution)/shard_map/reduce_scatter | solution.py:202
  568.0 148.0 %reduce-scatter.6.cloned.1.call-done = bf16[512,1024]{1,0:T(8,128)(2,1)} async-done(((bf16[4096,1024]{1,0:T(8,128)(2,1)}), bf16[512,1024]{1,0:T(8,128)(2,1)}) %reduce-scatter.6.cloned.1.call-update) | async-done | bytes 1048592 | tf_op jit(solution)/shard_map/reduce_scatter | solution.py:171
  724.6 17.2 %fusion.3 = (f32[8,2,512]{2,1,0:T(2,128)S(1)}, f32[8,512,512,2]{2,1,3,0:T(8,128)}) fusion(f32[8,2,512,512]{2,3,1,0:T(8,128)} %get-tuple-element.63, f32[8,2,512]{2,1,0:T(2,128)S(1)} %bitcast.243, bf16[512,8,64,1]{0,2,3,1:T(8,128)(2,1)} %bitcast.241, bf16[512,8,2,64]{0,3,2,1:T(8,128)(2,1)} %bitcast.219), kind=kOutput, calls=%fused_computation.8 | convolution fusion | flops 549445632 | bytes 35192832 | tf_op jit(solution)/shard_map/qgrd,kgd->grqk/dot_general | solution.py:248
  741.9 11.0 %fusion.5 = bf16[8,2,512,512]{2,3,1,0:T(8,128)(2,1)} fusion(f32[8,512,512,2]{2,1,3,0:T(8,128)} %get-tuple-element.72, f32[8,2,512,512]{2,3,1,0:T(8,128)S(1)} %bitcast.218, f32[8,2,512]{2,1,0:T(2,128)S(1)} %get-tuple-element.71, f32[8,2,512]{2,1,0:T(2,128)S(1)} %bitcast.244), kind=kLoop, calls=%fused_computation.10 | loop fusion | flops 16777216 | bytes 42008576 | tf_op jit(solution)/shard_map/convert_element_type | solution.py:253
  752.9 6.1 fusion.95
  759.3 5.2 convolution_multiply_fusion
  769.7 5.4 fusion.96
  775.2 5.8 fusion.88
  794.1 15.5 %reduce-scatter.12.cloned.1.call-done = bf16[4,256,512]{2,1,0:T(8,128)(2,1)} async-done(((bf16[4,1024,512]{2,1,0:T(8,128)(2,1)}), bf16[4,256,512]{2,1,0:T(8,128)(2,1)}) %reduce-scatter.12.cloned.1.call-update) | async-done | bytes 1048592 | tf_op jit(solution)/shard_map/reduce_scatter | solution.py:221
  812.4 44.8 %reduce-scatter.10.cloned.1.call-done = bf16[4,256,512]{2,1,0:T(8,128)(2,1)} async-done(((bf16[4,1024,512]{2,1,0:T(8,128)(2,1)}), bf16[4,256,512]{2,1,0:T(8,128)(2,1)}) %reduce-scatter.10.cloned.1.call-update) | async-done | bytes 1048592 | tf_op jit(solution)/shard_map/reduce_scatter | solution.py:218
  863.8 161.7 %all-reduce.3.cloned.1.call-done = (bf16[1024,128]{0,1:T(8,128)(2,1)}, bf16[1024,1024]{1,0:T(8,128)(2,1)}, bf16[1024,512]{1,0:T(8,128)(2,1)}, bf16[1024,512]{1,0:T(8,128)(2,1)}, bf16[1024,1024]{1,0:T(8,128)(2,1)}) async-done(((bf16[1024,128]{0,1:T(8,128)(2,1)}, bf16[1024,1024]{1,0:T(8,128)(2,1)}, bf16[1024,512]{1,0:T(8,128)(2,1)}, bf16[1024,512]{1,0:T(8,128)(2,1)}, bf16[1024,1024]{1,0:T(8,128)(2,1)}), ...) | async-done | bytes 6553616 | tf_op jit(solution)/shard_map/psum | solution.py:302
  (188 shorter events, 76.0 us)
Async XLA Ops:
  7.2 34.5 %copy-start = (bf16[1024,1024]{1,0:T(8,128)(2,1)S(1)}, bf16[1024,1024]{1,0:T(8,128)(2,1)}, u32[]{:S(2)}) copy-start(bf16[1024,1024]{1,0:T(8,128)(2,1)} %param.21) | copy-start | bytes 6291460
  7.2 130.6 %all-gather.6.cloned.1.call-start = ((), (), s32[]{:S(2)}) async-start(), calls=%async_computation.11 | async-start | bytes 9437184 | tf_op jit(solution)/shard_map/all_gather | solution.py:94
  8.0 256.3 %all-gather.8.cloned.1.call-start = ((), (), s32[]{:S(2)}) async-start(), calls=%async_computation.12 | async-start | bytes 9437184 | tf_op jit(solution)/shard_map/all_gather | solution.py:137
  16.9 8.7 copy-start.8
  16.9 8.7 copy-start.10
  17.8 16.2 %copy-start.31 = (bf16[512,512]{0,1:T(8,128)(2,1)}, bf16[512,512]{0,1:T(8,128)(2,1)S(1)}, u32[]{:S(2)}) copy-start(bf16[512,512]{0,1:T(8,128)(2,1)S(1)} %convolution_convert_fusion.5) | copy-start | bytes 1572868
  25.6 8.4 copy-start.34
  41.6 96.3 %copy-start.46 = (s32[512,8]{0,1:T(8,128)S(1)}, s32[512,8]{0,1:T(8,128)}, u32[]{:S(2)}) copy-start(s32[512,8]{0,1:T(8,128)} %param.16) | copy-start | bytes 49156
  137.9 426.2 %reduce-scatter.8.cloned.1.call-start = ((), (), s32[]{:S(2)}) async-start(), calls=%async_computation.7 | async-start | bytes 9437184 | tf_op jit(solution)/shard_map/reduce_scatter | solution.py:202
  170.4 93.8 %copy-start.32 = (bf16[1024,32]{0,1:T(8,128)(2,1)S(1)}, bf16[1024,32]{0,1:T(8,128)(2,1)}, u32[]{:S(2)}) copy-start(bf16[1024,32]{0,1:T(8,128)(2,1)} %param.23) | copy-start | bytes 196612
  271.2 13.1 %copy-start.47 = (bf16[4,1024,512]{2,1,0:T(8,128)(2,1)S(1)}, bf16[4,1024,512]{2,1,0:T(8,128)(2,1)}, u32[]{:S(2)}) copy-start(bf16[4,1024,512]{2,1,0:T(8,128)(2,1)} %param.24) | copy-start | bytes 12582916
  415.4 300.6 %reduce-scatter.6.cloned.1.call-start = ((), (), s32[]{:S(2)}) async-start(), calls=%async_computation.6 | async-start | bytes 9437184 | tf_op jit(solution)/shard_map/reduce_scatter | solution.py:171
  415.9 375.3 %reduce-scatter.14.cloned.1.call-start = ((), (), s32[]{:S(2)}) async-start(), calls=%async_computation.10 | async-start | bytes 5242880 | tf_op jit(solution)/shard_map/reduce_scatter | solution.py:224
  428.5 13.1 %copy-start.35 = (f32[8,2,512]{2,1,0:T(2,128)S(1)}, f32[8,2,512]{2,1,0:T(2,128)}, u32[]{:S(2)}) copy-start(f32[8,2,512]{2,1,0:T(2,128)} %copy-done.34) | copy-start | bytes 98308
  428.5 13.1 %copy-start.37 = (f32[8,2,512]{2,1,0:T(2,128)S(1)}, f32[8,2,512]{2,1,0:T(2,128)}, u32[]{:S(2)}) copy-start(f32[8,2,512]{2,1,0:T(2,128)} %copy-done.36) | copy-start | bytes 98308
  428.5 381.0 %reduce-scatter.12.cloned.1.call-start = ((), (), s32[]{:S(2)}) async-start(), calls=%async_computation.9 | async-start | bytes 5242880 | tf_op jit(solution)/shard_map/reduce_scatter | solution.py:221
  441.6 16.5 %all-to-all-start = ((f32[8,4,512]{2,1,0:T(4,128)}), f32[8,4,512]{2,1,0:T(4,128)S(1)}, u32[]{:S(2)}, u32[]{:S(2)}) async-start(f32[8,4,512]{2,1,0:T(4,128)} %get-tuple-element.36), calls=%async_computation.1 | async-start | bytes 131072 | tf_op jit(solution)/shard_map/all_to_all | solution.py:181
  445.0 14.9 %copy-start.4 = (bf16[512,1024]{1,0:T(8,128)(2,1)S(1)}, bf16[512,1024]{1,0:T(8,128)(2,1)}, u32[]{:S(2)}) copy-start(bf16[512,1024]{1,0:T(8,128)(2,1)} %multiply_convert_fusion) | copy-start | bytes 3145732
  445.0 119.0 %copy-start.33 = (bf16[1024,32]{0,1:T(8,128)(2,1)S(1)}, bf16[1024,32]{0,1:T(8,128)(2,1)}, u32[]{:S(2)}) copy-start(bf16[1024,32]{0,1:T(8,128)(2,1)} %param.23) | copy-start | bytes 196612
  445.0 119.0 %copy-start.39 = (f32[1024]{0:T(1024)S(1)}, f32[1024]{0:T(1024)}, u32[]{:S(2)}) copy-start(f32[1024]{0:T(1024)} %param.22) | copy-start | bytes 12292
  445.1 119.0 %copy-start.41 = (f32[512]{0:T(512)S(1)}, f32[512]{0:T(512)}, u32[]{:S(2)}) copy-start(f32[512]{0:T(512)} %copy-done.40) | copy-start | bytes 6148
  445.1 412.1 %reduce-scatter.10.cloned.1.call-start = ((), (), s32[]{:S(2)}) async-start(), calls=%async_computation.8 | async-start | bytes 5242880 | tf_op jit(solution)/shard_map/reduce_scatter | solution.py:218
  458.1 567.4 %all-reduce.3.cloned.1.call-start = ((), (), s32[]{:S(2)}) async-start(), calls=%async_computation.13 | async-start | bytes 13107200 | tf_op jit(solution)/shard_map/psum | solution.py:302
  724.6 17.2 %slice-start = ((s8[16777216]{0:T(1024)(128)(4,1)}), s8[4194304]{0:T(1024)(128)(4,1)S(1)}, s32[]{:S(2)}) async-start(s8[16777216]{0:T(1024)(128)(4,1)} %bitcast.217), calls=%async_computation.14 | async-start | bytes 8388608
  724.6 17.2 %slice-start.1 = ((s8[16777216]{0:T(1024)(128)(4,1)}), s8[4194304]{0:T(1024)(128)(4,1)S(1)}, s32[]{:S(2)}) async-start(s8[16777216]{0:T(1024)(128)(4,1)} %bitcast.217), calls=%async_computation.15 | async-start | bytes 8388608
  724.6 17.2 %slice-start.2 = ((s8[16777216]{0:T(1024)(128)(4,1)}), s8[4194304]{0:T(1024)(128)(4,1)S(1)}, s32[]{:S(2)}) async-start(s8[16777216]{0:T(1024)(128)(4,1)} %bitcast.217), calls=%async_computation.16 | async-start | bytes 8388608
  724.6 17.2 %slice-start.3 = ((s8[16777216]{0:T(1024)(128)(4,1)}), s8[4194304]{0:T(1024)(128)(4,1)S(1)}, s32[]{:S(2)}) async-start(s8[16777216]{0:T(1024)(128)(4,1)} %bitcast.217), calls=%async_computation.17 | async-start | bytes 8388608
  741.9 11.0 %copy-start.9 = (bf16[512,16,32]{0,2,1:T(8,128)(2,1)S(1)}, bf16[512,16,32]{0,2,1:T(8,128)(2,1)}, u32[]{:S(2)}) copy-start(bf16[512,16,32]{0,2,1:T(8,128)(2,1)} %copy-done.8) | copy-start | bytes 1572868
  741.9 11.0 %copy-start.11 = (bf16[512,16,32]{0,2,1:T(8,128)(2,1)S(1)}, bf16[512,16,32]{0,2,1:T(8,128)(2,1)}, u32[]{:S(2)}) copy-start(bf16[512,16,32]{0,2,1:T(8,128)(2,1)} %copy-done.10) | copy-start | bytes 1572868
  775.1 8.7 copy-start.14
  775.2 10.6 %copy-start.21 = (bf16[512,16,64]{0,2,1:T(8,128)(2,1)S(1)}, bf16[512,16,64]{0,2,1:T(8,128)(2,1)}, u32[]{:S(2)}) copy-start(bf16[512,16,64]{0,2,1:T(8,128)(2,1)} %copy-done.20) | copy-start | bytes 3145732
  1025.5 8.8 copy-start.18
  (31 other events, 149.0 us)
Sparse Core Ops, SparseCore 0:
  10.2 127.6 all-gather.5
  140.5 123.7 all-gather.7
  415.5 148.4 reduce-scatter.7
  568.0 147.9 reduce-scatter.5
  718.4 43.4 reduce-scatter.13
  765.0 44.5 reduce-scatter.11
  812.7 44.4 reduce-scatter.9
  864.8 160.6 all-reduce.2
